TPU v7x, 128 devices: a whole 4x4x4 slice. The times are simulated.
128 devices in a mesh: dp: 16 (over x_hi, y, core), seq: 8 (over z, x_lo).
Axes of the slice: x: 4 (x_hi: 2, x_lo: 2; x = x_hi * 2 + x_lo), y: 4, z: 4, core: 2. Of those that a mesh axis runs over, the one named last changes fastest.
Arguments:
- bases: int32 [16, 8192], P('dp', 'seq'), may hold values from 0 to 3
- upsampled: bfloat16 [16, 8192, 768], P('dp', 'seq'), may hold values from -6 to 6
- base_table: bfloat16 [4, 768], replicated, may hold values from -4 to 4
- filter_weight: bfloat16 [5, 768, 768], replicated, may hold values from -0.09375 to 0.09375
- filter_bias: float32 [768], replicated, may hold values from -3 to 3
- norm_gain: float32 [768], replicated, may hold values from 0.5 to 1.5
- cotangent: bfloat16 [16, 8192, 768], P('dp', 'seq'), may hold values from -6 to 6
Outputs:
- block_out: bfloat16 [16, 8192, 768], P('dp', 'seq')
- grad_input: bfloat16 [16, 8192, 768], P('dp', 'seq')
- grad_weight: float32 [5, 768, 768], P(None, ('dp', 'seq'))
- grad_bias: float32 [768], P(('dp', 'seq'))
- grad_gain: float32 [768], P(('dp', 'seq'))
All inputs are finite; a program needn't handle non-finite values.
Results may differ from a plain program's by a relative error of at most 0.0085.
Values may be sent and summed in bfloat16 or wider, within the bound.
A program may use at most 128 MiB of HBM per device.

v0:
```python
import jax
import jax.numpy as jnp
from jax import lax
from jax.sharding import PartitionSpec as P

DILATION_STEP = 4


def extended(cells, sides, width):
    for axis, dim in sides:
        count = lax.axis_size(axis)
        ends = count - 1
        head = lax.slice_in_dim(cells, 0, width, axis=dim)
        tail = lax.slice_in_dim(cells, cells.shape[dim] - width, cells.shape[dim], axis=dim)
        cells = jnp.concatenate(
            [
                lax.ppermute(tail, axis, [(i, (i + 1) % count) for i in range(ends)]),
                cells,
                lax.ppermute(head, axis, [((i + 1) % count, i) for i in range(ends)]),
            ],
            axis=dim,
        )
    return cells


def embed_norm(onehot, up_rows, base_table, norm_gain):
    x = up_rows.astype(jnp.float32) + jnp.dot(
        onehot, base_table, preferred_element_type=jnp.float32
    )
    rms = jnp.sqrt(jnp.mean(x * x, axis=-1, keepdims=True) + 1e-06)
    normed = x / rms
    h = (normed * norm_gain).astype(jnp.bfloat16)
    return (x, rms, normed, h)


def body(bases, upsampled, base_table, filter_weight, filter_bias, norm_gain, cotangent):
    taps = filter_weight.shape[0]
    middle_tap = (taps - 1) // 2
    channel_width = middle_tap * DILATION_STEP
    input_rows = upsampled.shape[1]
    onehot = (bases[0][:, None] == jnp.arange(4, dtype=jnp.int32)[None, :]).astype(jnp.bfloat16)
    x, rms, normed, h = embed_norm(onehot, upsampled[0], base_table, norm_gain)
    padded_input = extended(h, (("seq", 0),), channel_width)
    preactivation = filter_bias[None, :] + sum(
        (
            jnp.dot(
                padded_input[tap_index * DILATION_STEP : tap_index * DILATION_STEP + input_rows],
                filter_weight[tap_index],
                preferred_element_type=jnp.float32,
            )
            for tap_index in range(taps)
        )
    )
    act, pull = jax.vjp(jax.nn.gelu, preactivation)
    block_out = (x + act).astype(jnp.bfloat16)
    cot_rows = cotangent[0]
    output_gradient = pull(cot_rows.astype(jnp.float32))[0].astype(jnp.bfloat16)
    padded_gradient = extended(output_gradient, (("seq", 0),), channel_width)
    weight_gradient = jnp.stack(
        [
            jnp.einsum(
                "as,af->sf",
                padded_input[tap_index * DILATION_STEP : tap_index * DILATION_STEP + input_rows],
                output_gradient,
                preferred_element_type=jnp.float32,
            )
            for tap_index in range(taps)
        ]
    )
    dbias = jnp.sum(output_gradient.astype(jnp.float32), axis=0)
    hidden_gradient = sum(
        (
            jnp.einsum(
                "to,io->ti",
                padded_gradient[
                    (2 * middle_tap - tap_index)
                    * DILATION_STEP : (2 * middle_tap - tap_index)
                    * DILATION_STEP
                    + input_rows
                ],
                filter_weight[tap_index],
                preferred_element_type=jnp.float32,
            )
            for tap_index in range(taps)
        )
    )
    dgain = jnp.sum(hidden_gradient * normed, axis=0)
    grad_weight, grad_bias, grad_gain = (
        lax.psum_scatter(weight_gradient, ("dp", "seq"), scatter_dimension=1, tiled=True),
        lax.psum_scatter(dbias, ("dp", "seq"), scatter_dimension=0, tiled=True),
        lax.psum_scatter(dgain, ("dp", "seq"), scatter_dimension=0, tiled=True),
    )
    dn = hidden_gradient * norm_gain
    grad_in = (
        cot_rows.astype(jnp.float32)
        + (dn - normed * jnp.mean(dn * normed, axis=-1, keepdims=True)) / rms
    )
    return (block_out[None], grad_in.astype(jnp.bfloat16)[None], grad_weight, grad_bias, grad_gain)


def solution(mesh):
    placed = (P("dp", "seq"), P("dp", "seq", None), P(), P(), P(), P(), P("dp", "seq", None))
    return jax.shard_map(
        body,
        mesh=mesh,
        in_specs=placed,
        out_specs=(
            P("dp", "seq", None),
            P("dp", "seq", None),
            P(None, ("dp", "seq"), None),
            P(("dp", "seq")),
            P(("dp", "seq")),
        ),
        check_vma=False,
    )
```

profile of v0, /device:TPU:0, one launch (start us, length us, event | category | flops | bytes accessed | tf_op | source)
XLA Modules:
  0.0 221.7 jit_solution(16834019069110154036)
XLA Ops:
  7.9 2.3 %multiply_reduce_fusion.2 = (f32[1024]{0:T(1024)S(1)}, f32[1024,768]{1,0:T(8,128)S(1)}) fusion(bf16[4,768]{1,0:T(4,128)(2,1)S(1)} %copy-done, s32[1024]{0:T(1024)} %bitcast.69, bf16[1,1024,768]{2,1,0:T(8,128)(2,1)} %param.8), kind=kOutput, calls=%fused_computation.24 | convolution fusion | flops 9440256 | bytes 4732928 | tf_op jit(solution)/shard_map/dot_general | solution.py:27
  10.6 3.5 %collective-permute-start = (bf16[8,768]{1,0:T(8,128)(2,1)S(1)}, bf16[8,768]{1,0:T(8,128)(2,1)S(1)}, u32[]{:S(2)}, u32[]{:S(2)}) collective-permute-start(bf16[8,768]{1,0:T(8,128)(2,1)S(1)} %get-tuple-element.15), channel_id=1, source_target_pairs={{0,1},{1,2},{2,3},{3,4},{4,5},{5,6},{6,7},{8,9},{9,10},{10,11},{11... | collective-permute-start | bytes 36872 | tf_op jit(solution)/shard_map/ppermute | solution.py:17
  14.1 1.3 collective-permute-start.1
  15.4 1.4 fusion.33
  16.8 1.4 fusion.39
  18.2 1.4 fusion.36
  19.7 1.4 fusion.29
  21.2 5.5 %convert_reduce_fusion = (f32[768]{0:T(1024)S(1)}, bf16[1024,768]{1,0:T(8,128)(2,1)S(1)}, f32[1024,768]{1,0:T(8,128)}) fusion(bf16[1,1024,768]{2,1,0:T(8,128)(2,1)S(1)} %copy-done.2, bf16[5,768,768]{2,1,0:T(8,128)(2,1)S(1)} %copy-done.6, bf16[8,768]{1,0:T(8,128)(2,1)S(1)} %collective-permute-done.1, bf16[1024,768]{1,0:T(8,128)(2,1)S(1)} %multiply_convert_fusion, ...), kind=kOutput, calls=%fused_computation.18 | convolution fusion | flops 1233124608 | bytes 21646336 | tf_op jit(solution)/shard_map/dot_general | solution.py:46
  26.6 2.9 %bitcast_dynamic-update-slice_fusion.4 = f32[5,768,768]{2,1,0:T(8,128)} fusion(bf16[1024,768]{1,0:T(8,128)(2,1)S(1)} %get-tuple-element.10, bf16[8,768]{1,0:T(8,128)(2,1)S(1)} %collective-permute-done, bf16[1024,768]{1,0:T(8,128)(2,1)S(1)} %multiply_convert_fusion), kind=kOutput, calls=%fused_computation.29 | convolution fusion | flops 1211105280 | bytes 5517312 | tf_op jit(solution)/shard_map/as,af->sf/dot_general | solution.py:61
  29.5 2.8 %bitcast_dynamic-update-slice_fusion.3 = f32[5,768,768]{2,1,0:T(8,128)} fusion(f32[5,768,768]{2,1,0:T(8,128)} %bitcast_dynamic-update-slice_fusion.4, bf16[1024,768]{1,0:T(8,128)(2,1)S(1)} %get-tuple-element.10, bf16[1024,768]{1,0:T(8,128)(2,1)S(1)} %multiply_convert_fusion, bf16[8,768]{1,0:T(8,128)(2,1)S(1)} %collective-permute-done), kind=kOutput, calls=%fused_computation.28 | convolution fusion | flops 1211105280 | bytes 5517312 | tf_op jit(solution)/shard_map/as,af->sf/dot_general | solution.py:61
  32.4 2.9 %bitcast_dynamic-update-slice_fusion.2 = f32[5,768,768]{2,1,0:T(8,128)} fusion(f32[5,768,768]{2,1,0:T(8,128)} %bitcast_dynamic-update-slice_fusion.3, bf16[1024,768]{1,0:T(8,128)(2,1)S(1)} %multiply_convert_fusion, bf16[1024,768]{1,0:T(8,128)(2,1)S(1)} %get-tuple-element.10), kind=kOutput, calls=%fused_computation.27 | convolution fusion | flops 1207959552 | bytes 5505024 | tf_op jit(solution)/shard_map/as,af->sf/dot_general | solution.py:61
  35.2 2.8 %bitcast_dynamic-update-slice_fusion.1 = f32[5,768,768]{2,1,0:T(8,128)} fusion(f32[5,768,768]{2,1,0:T(8,128)} %bitcast_dynamic-update-slice_fusion.2, bf16[1024,768]{1,0:T(8,128)(2,1)S(1)} %get-tuple-element.10, bf16[1024,768]{1,0:T(8,128)(2,1)S(1)} %multiply_convert_fusion, bf16[8,768]{1,0:T(8,128)(2,1)S(1)} %collective-permute-done.1), kind=kOutput, calls=%fused_computation.26 | convolution fusion | flops 1211105280 | bytes 5517312 | tf_op jit(solution)/shard_map/as,af->sf/dot_general | solution.py:61
  38.1 2.9 %bitcast_dynamic-update-slice_fusion = f32[5,768,768]{2,1,0:T(8,128)} fusion(f32[5,768,768]{2,1,0:T(8,128)} %bitcast_dynamic-update-slice_fusion.1, bf16[1024,768]{1,0:T(8,128)(2,1)S(1)} %get-tuple-element.10, bf16[8,768]{1,0:T(8,128)(2,1)S(1)} %collective-permute-done.1, bf16[1024,768]{1,0:T(8,128)(2,1)S(1)} %multiply_convert_fusion), kind=kOutput, calls=%fused_computation.25 | convolution fusion | flops 1211105280 | bytes 5517312 | tf_op jit(solution)/shard_map/as,af->sf/dot_general | solution.py:61
  41.7 1.4 collective-permute-start.2
  43.2 3.2 %fusion.31 = f32[1024,768]{1,0:T(8,128)S(1)} fusion(bf16[1024,768]{1,0:T(8,128)(2,1)} %copy-done.4, bf16[5,768,768]{2,1,0:T(8,128)(2,1)} %param.10), kind=kOutput, calls=%fused_computation.61 | convolution fusion | flops 1207959552 | bytes 5898240 | tf_op jit(solution)/shard_map/to,io->ti/dot_general | solution.py:73
  46.4 5.8 %collective-permute-start.3 = (bf16[8,768]{1,0:T(8,128)(2,1)S(1)}, bf16[8,768]{1,0:T(8,128)(2,1)S(1)}, u32[]{:S(2)}, u32[]{:S(2)}) collective-permute-start(bf16[8,768]{1,0:T(8,128)(2,1)S(1)} %get-tuple-element.14), channel_id=1, source_target_pairs={{0,1},{1,2},{2,3},{3,4},{4,5},{5,6},{6,7},{8,9},{9,10},{10,11},{11... | collective-permute-start | bytes 36872 | tf_op jit(solution)/shard_map/ppermute | solution.py:17
  52.2 2.7 %fusion.15 = f32[1024,768]{1,0:T(8,128)S(1)} fusion(bf16[1024,768]{1,0:T(8,128)(2,1)S(1)} %copy-done.5, bf16[8,768]{1,0:T(8,128)(2,1)S(1)} %collective-permute-done.2, bf16[5,768,768]{2,1,0:T(8,128)(2,1)} %param.10), kind=kOutput, calls=%fused_computation.41 | convolution fusion | flops 1211105280 | bytes 5910528 | tf_op jit(solution)/shard_map/to,io->ti/dot_general | solution.py:73
  55.0 1.4 fusion.21
  56.4 1.5 fusion.12
  57.9 4.1 %multiply_reduce_fusion = (f32[768]{0:T(1024)S(1)}, f32[1024]{0:T(1024)S(1)}, f32[1024,768]{1,0:T(8,128)}) fusion(f32[1024,768]{1,0:T(8,128)S(1)} %get-tuple-element.18, f32[1024]{0:T(1024)S(1)} %add_sqrt_fusion, f32[768]{0:T(1024)S(1)} %copy-done.3, bf16[5,768,768]{2,1,0:T(8,128)(2,1)S(1)} %bitcast.71, bf16[1024,768]{1,0:T(8,128)(2,1)S(1)} %copy-done.5, ...), kind=kOutput, calls=%fused_computation.17 | convolution fusion | flops 1218967808 | bytes 21654528 | tf_op jit(solution)/shard_map/to,io->ti/dot_general | solution.py:73
  62.0 68.2 %all-reduce.3 = (f32[768]{0:T(1024)S(1)}, f32[768]{0:T(1024)S(1)}) all-reduce(f32[768]{0:T(1024)S(1)} %get-tuple-element.9, f32[768]{0:T(1024)S(1)} %get-tuple-element.5), channel_id=3, replica_groups=mesh['dp'=16,'seq'=8] {'dp','seq'}, use_global_device_ids=true, to_apply=%region_4.0.clone | all-reduce | flops 1536 | bytes 12288
  131.4 5.5 %fusion.24 = (bf16[1,1024,768]{2,1,0:T(8,128)(2,1)}, bf16[1,1024,768]{2,1,0:T(8,128)(2,1)}) fusion(f32[1024]{0:T(1024)S(1)} %add_sqrt_fusion, f32[1024]{0:T(1024)S(1)} %broadcast_multiply_fusion, f32[1024,768]{1,0:T(8,128)} %get-tuple-element.20, f32[768]{0:T(1024)S(1)} %copy-done.3, bf16[1,1024,768]{2,1,0:T(8,128)(2,1)} %param.13, ...), kind=kLoop, calls=%fused_computation.54 | loop fusion | flops 14155776 | bytes 14167040 | tf_op jit(solution)/shard_map/broadcast_in_dim | solution.py:98
  136.9 76.3 %all-reduce.6.cloned.1.call-done = f32[5,768,768]{2,1,0:T(8,128)} async-done(((f32[5,768,768]{2,1,0:T(8,128)}), f32[5,768,768]{2,1,0:T(8,128)}) %all-reduce.6.cloned.1.call-update) | async-done | bytes 11796496
  213.2 1.6 constant_dynamic-slice_fusion
  (34 shorter events, 3.0 us)
Async XLA Ops:
  7.2 0.7 copy-start
  7.2 3.1 %copy-start.3 = (f32[768]{0:T(1024)S(1)}, f32[768]{0:T(1024)}, u32[]{:S(2)}) copy-start(f32[768]{0:T(1024)} %param.12) | copy-start | bytes 9220
  7.2 206.0 %all-reduce.6.cloned.1.call-start = ((), (), s32[]{:S(2)}) async-start(), calls=%async_computation | async-start | bytes 23592960
  7.9 7.6 %copy-start.6 = (bf16[5,768,768]{2,1,0:T(8,128)(2,1)S(1)}, bf16[5,768,768]{2,1,0:T(8,128)(2,1)}, u32[]{:S(2)}) copy-start(bf16[5,768,768]{2,1,0:T(8,128)(2,1)} %param.10) | copy-start | bytes 17694724
  10.6 6.2 %collective-permute-start = (bf16[8,768]{1,0:T(8,128)(2,1)S(1)}, bf16[8,768]{1,0:T(8,128)(2,1)S(1)}, u32[]{:S(2)}, u32[]{:S(2)}) collective-permute-start(bf16[8,768]{1,0:T(8,128)(2,1)S(1)} %get-tuple-element.15), channel_id=1, source_target_pairs={{0,1},{1,2},{2,3},{3,4},{4,5},{5,6},{6,7},{8,9},{9,10},{10,11},{11... | collective-permute-start | bytes 36872 | tf_op jit(solution)/shard_map/ppermute | solution.py:17
  14.1 5.6 %collective-permute-start.1 = (bf16[8,768]{1,0:T(8,128)(2,1)S(1)}, bf16[8,768]{1,0:T(8,128)(2,1)S(1)}, u32[]{:S(2)}, u32[]{:S(2)}) collective-permute-start(bf16[8,768]{1,0:T(8,128)(2,1)S(1)} %get-tuple-element.16), channel_id=1, source_target_pairs={{1,0},{2,1},{3,2},{4,3},{5,4},{6,5},{7,6},{9,8},{10,9},{11,10},{12... | collective-permute-start | bytes 36872 | tf_op jit(solution)/shard_map/ppermute | solution.py:19
  19.7 1.5 copy-start.2
  19.7 1.5 copy-start.7
  26.6 11.5 %copy-start.4 = (bf16[1024,768]{1,0:T(8,128)(2,1)}, bf16[1024,768]{1,0:T(8,128)(2,1)S(1)}, u32[]{:S(2)}) copy-start(bf16[1024,768]{1,0:T(8,128)(2,1)S(1)} %get-tuple-element.10) | copy-start | bytes 4718596
  41.7 10.5 %copy-start.5 = (bf16[1024,768]{1,0:T(8,128)(2,1)S(1)}, bf16[1024,768]{1,0:T(8,128)(2,1)}, u32[]{:S(2)}) copy-start(bf16[1024,768]{1,0:T(8,128)(2,1)} %copy-done.4) | copy-start | bytes 4718596
  41.7 10.5 %collective-permute-start.2 = (bf16[8,768]{1,0:T(8,128)(2,1)S(1)}, bf16[8,768]{1,0:T(8,128)(2,1)S(1)}, u32[]{:S(2)}, u32[]{:S(2)}) collective-permute-start(bf16[8,768]{1,0:T(8,128)(2,1)S(1)} %get-tuple-element.13), channel_id=1, source_target_pairs={{1,0},{2,1},{3,2},{4,3},{5,4},{6,5},{7,6},{9,8},{10,9},{11,10},{12... | collective-permute-start | bytes 36872 | tf_op jit(solution)/shard_map/ppermute | solution.py:19
  46.3 8.6 %slice-start = ((s8[5898240]{0:T(1024)(128)(4,1)}), s8[4194304]{0:T(1024)(128)(4,1)S(1)}, s32[]{:S(2)}) async-start(s8[5898240]{0:T(1024)(128)(4,1)} %bitcast.70), calls=%async_computation.1 | async-start | bytes 8388608
  46.4 8.6 %slice-start.1 = ((s8[5898240]{0:T(1024)(128)(4,1)}), s8[1703936]{0:T(1024)(128)(4,1)S(1)}, s32[]{:S(2)}) async-start(s8[5898240]{0:T(1024)(128)(4,1)} %bitcast.70), calls=%async_computation.2 | async-start | bytes 3407872
  46.4 10.0 %collective-permute-start.3 = (bf16[8,768]{1,0:T(8,128)(2,1)S(1)}, bf16[8,768]{1,0:T(8,128)(2,1)S(1)}, u32[]{:S(2)}, u32[]{:S(2)}) collective-permute-start(bf16[8,768]{1,0:T(8,128)(2,1)S(1)} %get-tuple-element.14), channel_id=1, source_target_pairs={{0,1},{1,2},{2,3},{3,4},{4,5},{5,6},{6,7},{8,9},{9,10},{10,11},{11... | collective-permute-start | bytes 36872 | tf_op jit(solution)/shard_map/ppermute | solution.py:17
  131.4 83.5 %copy-start.1 = (bf16[4,768]{1,0:T(4,128)(2,1)S(1)}, bf16[4,768]{1,0:T(4,128)(2,1)}, u32[]{:S(2)}) copy-start(bf16[4,768]{1,0:T(4,128)(2,1)} %param.9) | copy-start | bytes 18436
Sparse Core Ops, SparseCore 0:
  41.1 172.0 all-reduce.5
where the time goes:
time: 223 us; the launch traced here: 222 us
  waiting for transfers between devices  76.3 us (34%)
  blocking collectives  68.2 us (31%)
  matrix products  40.7 us (18%)
  between operations  14.3 us (6%)
  starting transfers between devices  12 us (5%)
  other arithmetic  5.92 us (3%)
  local copies, waits for them, and re-layouts  4.19 us (2%)
    unnamed x2, waiting for transfers between devices  76.3 us
    unnamed x1, blocking collectives  68.2 us
    dot_general x5, matrix products, body(): jnp.einsum('as,af->sf', padded_input[tap_index * DILATION_STEP:tap_index...  14.4 us
    dot_general x5, matrix products, body(): jnp.einsum('to,io->ti', padded_gradient[(2 * middle_tap - tap_index) * DI...  12.9 us
    dot_general x5, matrix products, body(): jnp.dot(padded_input[tap_index * DILATION_STEP:tap_index * DILATION_STEP...  11.1 us
    ppermute x2, starting transfers between devices, extended(): lax.ppermute(tail, axis, [(i, (i + 1) % count) for i in range(ends)])  9.3 us
    broadcast_in_dim x1, other arithmetic, body(): grad_in.astype(jnp.bfloat16)[None]  5.54 us
  transfers between devices with their start and end apart: 5, of which 1 were waited for; matrix products, arithmetic and copies ran while one was open for 11% of the time, Pallas kernels for 0%

commit v1 on v0

v1 whole, which is shorter than its diff:
```python
import jax
import jax.numpy as jnp
import numpy as np
from jax import lax
from jax.experimental import pallas as pl
from jax.experimental.pallas import tpu as pltpu
from jax.sharding import PartitionSpec as P

BF, F32 = jnp.bfloat16, jnp.float32
C, TAPS, STEP = 768, 5, 4
ROWS, HALO = 1024, 16
EXT = ROWS + 2 * HALO
WIDE = 256
GROUPS = C // WIDE
HALF = C // 2
NT = (((1,), (1,)), ((), ()))
TN = (((0,), (0,)), ((), ()))

ORDERS = ((0, 1, 2), (1, 0, 2), (2, 0, 1))
PIECES = [
    (group, kind, [k for k in range(TAPS) if (k + group) % 3 == kind])
    for group in range(GROUPS)
    for kind in ((0, 1, 2) if group < 2 else (0, 2, 1))
]
BIAS_PIECE = next(q for q, (group, kind, taps) in enumerate(PIECES) if group == 2 and len(taps) == 1)


def width(q):
    return WIDE * len(PIECES[q][2]) + (128 if q == BIAS_PIECE else 0)


def permutations():
    perm = np.zeros((C, C), np.float32)
    perm_z = np.zeros((HALF, HALF), np.float32)
    for core in range(2):
        for x in range(4):
            for y in range(4):
                for z in range(4):
                    for j in range(6):
                        row = ((x * 4 + y) * 4 + z) * 6 + j
                        source = (x // 2) * 384 + y * 96 + core * 48 + z * 12 + (x % 2) * 6 + j
                        perm[core * HALF + row, source] = 1
                        perm_z[((z * 4 + x) * 4 + y) * 6 + j, row] = 1
    return perm, perm_z


def here():
    dp, seq = lax.axis_index("dp"), lax.axis_index("seq")
    x = 2 * lax.div(dp, 8) + lax.rem(seq, 2)
    return [x, lax.rem(lax.div(dp, 2), 4), lax.div(seq, 2)], lax.rem(dp, 2), dp, seq


def place(pos, core):
    x, y, z = pos
    return (lax.div(x, 2) * 8 + y * 2 + core, z * 2 + lax.rem(x, 2))


def moved(pos, axis, delta):
    other = list(pos)
    other[axis] = lax.rem(pos[axis] + delta, 4)
    return other


def kernel(*refs):
    names = iter(refs)

    def take(n):
        return [next(names) for _ in range(n)]

    bases, up, table, weight, bias, gain, cot, perm, perm_z = take(9)
    out, gin, gw, gbias, ggain = take(5)
    (bases_e, up_e, cot_e, w_v, perm_v, permz_v, tab, xs, rin, hb, h5, hT, hsend, pre) = take(14)
    gbuf, gpar, g5, g5p, bsum, ob, gi, dhs, gws = take(9)
    bufs = [take(6) for _ in PIECES]
    local_sem, send_sem, recv_sem = take(3)

    pos, core, dp, seq = here()
    partner = place(pos, 1 - core)
    left, right = (dp, lax.rem(seq + 7, 8)), (dp, lax.rem(seq + 1, 8))
    remote_count, local_count, started = [0], [0], []

    def remote(src, dst, device):
        n = remote_count[0]
        remote_count[0] += 1
        copy = pltpu.make_async_remote_copy(
            src_ref=src, dst_ref=dst, send_sem=send_sem.at[n], recv_sem=recv_sem.at[n],
            device_id=device, device_id_type=MESH,
        )
        copy.start()
        started.append(copy)
        return copy

    def local(src, dst):
        n = local_count[0]
        local_count[0] += 1
        copy = pltpu.make_async_copy(src, dst, local_sem.at[n])
        copy.start()
        return copy

    in_bases = local(bases, bases_e.at[:, pl.ds(128, ROWS)])
    in_up = local(up, up_e.at[pl.ds(HALO, ROWS)])
    in_perm = [
        local(perm.at[pl.ds(pl.multiple_of(c * HALF, HALF), HALF)], perm_v.at[pl.ds(half * HALF, HALF)])
        for half, c in enumerate((core, 1 - core))
    ]
    in_w = [local(weight.at[:, pl.ds(p * WIDE, WIDE)], w_v.at[:, pl.ds(p * WIDE, WIDE)]) for p in range(GROUPS)]
    in_cot = local(cot, cot_e.at[pl.ds(HALO, ROWS)])
    in_permz = local(perm_z, permz_v)

    barrier = pltpu.get_barrier_semaphore()
    partners = [partner, left, right]
    partners += [place(moved(pos, axis, delta), core) for axis in range(3) for delta in (1, 2, 3)]
    for device in partners:
        pl.semaphore_signal(barrier, inc=1, device_id=device, device_id_type=MESH)
    pl.semaphore_wait(barrier, len(partners))

    halos = [
        remote(bases.at[:, pl.ds(ROWS - 128, 128)], bases_e.at[:, pl.ds(0, 128)], right),
        remote(bases.at[:, pl.ds(0, 128)], bases_e.at[:, pl.ds(128 + ROWS, 128)], left),
    ]
    for source, target in ((up, up_e), (cot, cot_e)):
        halos += [
            remote(source.at[pl.ds(ROWS - HALO, HALO)], target.at[pl.ds(0, HALO)], right),
            remote(source.at[pl.ds(0, HALO)], target.at[pl.ds(HALO + ROWS, HALO)], left),
        ]

    tab[...] = jnp.zeros(tab.shape, F32)
    tab[0:4, :] = table[...].astype(F32)
    code = lax.broadcasted_iota(jnp.int32, (8, 128), 0)

    def embedded(block):
        onehot = (code == bases_e[:, pl.ds(pl.multiple_of(block * 128, 128), 128)]).astype(F32)
        return lax.dot_general(onehot, tab[...], TN, preferred_element_type=F32)

    def normed_of(x):
        r = lax.rsqrt(jnp.mean(x * x, axis=-1, keepdims=True) + 1e-06)
        return r, (x * r * gain[...])

    in_bases.wait()
    in_up.wait()

    def norm_block(b, carry):
        e = embedded(b + 1)
        for s in range(4):
            row = pl.multiple_of(b * 128 + s * 32, 32)
            x = up_e[pl.ds(row + HALO, 32), :].astype(F32) + e[s * 32 : s * 32 + 32]
            r, h = normed_of(x)
            xs[pl.ds(row, 32), :] = x
            rin[pl.ds(row, 32), :] = jnp.broadcast_to(r, (32, 128))
            hb[pl.ds(row + 2 * HALO, 32), :] = h.astype(BF)
        return carry

    lax.fori_loop(0, ROWS // 128, norm_block, 0)
    for copy in halos:
        copy.wait_recv()
    hb[0:HALO, :] = jnp.zeros((HALO, C), BF)
    hb[HALO + EXT : 2 * HALO + EXT, :] = jnp.zeros((HALO, C), BF)
    inside = (seq > 0, seq < 7)
    for side, (block, skip) in enumerate(((0, 128 - HALO), (1 + ROWS // 128, 0))):
        start = side * (HALO + ROWS)
        x = up_e[start : start + HALO, :].astype(F32) + embedded(block)[skip : skip + HALO]
        h = jnp.where(inside[side], normed_of(x)[1], 0.0)
        hb[start + HALO : start + 2 * HALO, :] = h.astype(BF)

    for copy in in_perm:
        copy.wait()
    h_own = hb[2 * HALO : 2 * HALO + ROWS, :]
    hsend[...] = lax.dot_general(perm_v[HALF:, :], h_own, NT, preferred_element_type=F32).astype(BF)
    h_copy = remote(hsend, hT.at[:, pl.ds(ROWS, ROWS)], partner)
    hT[:, 0:ROWS] = lax.dot_general(perm_v[0:HALF, :], h_own, NT, preferred_element_type=F32).astype(BF)

    def shift_h(j, carry):
        row = pl.multiple_of(j * 96, 32)
        for p in range(GROUPS):
            v = hb[pl.ds(row, 128), p * WIDE : (p + 1) * WIDE].astype(F32)
            for k in range(TAPS):
                h5[pl.ds(row, 96), k * C + p * WIDE : k * C + (p + 1) * WIDE] = v[8 + STEP * k : 104 + STEP * k].astype(BF)
        return carry

    lax.fori_loop(0, EXT // 96, shift_h, 0)
    bsum[...] = jnp.zeros(bsum.shape, F32)
    in_permz.wait()
    in_cot.wait()
    c0 = np.float32(np.sqrt(2 / np.pi))
    outgoing, g_copies = [], []

    def gelu_pair(z):
        square = z * z
        t = jnp.tanh(c0 * z * (1 + 0.044715 * square))
        cdf = 0.5 + 0.5 * t
        slope = cdf + (0.5 * c0) * z * (1 - t * t) * (1 + 0.134145 * square)
        return z * cdf, slope

    def forward(p):
        cols = slice(p * WIDE, (p + 1) * WIDE)
        in_w[p].wait()
        pre[...] = jnp.dot(h5[...], w_v[:, cols], preferred_element_type=F32)

        def tile(i, carry):
            row = pl.multiple_of(i * 64, 64)
            act, slope = gelu_pair(pre[pl.ds(row + HALO, 64), :] + bias[:, cols])
            ob[pl.ds(row, 64), cols] = (xs[pl.ds(row, 64), cols] + act).astype(BF)
            gbuf[p, pl.ds(row + HALO, 64), :] = (cot_e[pl.ds(row + HALO, 64), cols].astype(F32) * slope).astype(BF)
            return carry

        lax.fori_loop(0, ROWS // 64, tile, 0)
        for side in range(2):
            rows = slice(side * (HALO + ROWS), side * (HALO + ROWS) + HALO)
            _, slope = gelu_pair(pre[rows, :] + bias[:, cols])
            g = jnp.where(inside[side], cot_e[rows, cols].astype(F32) * slope, 0.0)
            gbuf[p, rows, :] = g.astype(BF)
        g_copies.append(remote(gbuf.at[p], gpar.at[p], partner))
        outgoing.append(local(ob.at[:, pl.ds(p * WIDE, WIDE)], out.at[:, pl.ds(p * WIDE, WIDE)]))

    def shift_g(source, p, target, column):
        def tile(j, total):
            row = pl.multiple_of(j * 128, 128)
            v = source[p, pl.ds(row, 160), :].astype(F32)
            for k in range(TAPS):
                col = column(k)
                target[pl.ds(row, 128), col : col + WIDE] = v[24 - STEP * k : 152 - STEP * k].astype(BF)
            return total + jnp.sum(v[16:144].reshape(16, 8, WIDE), axis=0)

        cols = slice(p * WIDE, (p + 1) * WIDE)
        bsum[:, cols] += lax.fori_loop(0, ROWS // 128, tile, jnp.zeros((8, WIDE), F32))

    hops = {}

    def send(q, stage):
        axis = ORDERS[PIECES[q][1]][stage]
        source, target = bufs[q][2 * stage], bufs[q][2 * stage + 1]
        hops[q, stage] = [
            remote(source.at[moved(pos, axis, delta)[axis]], target.at[delta - 1], place(moved(pos, axis, delta), core))
            for delta in (1, 2, 3)
        ]

    def store_first(q, r, col, n):
        kind, target = PIECES[q][1], bufs[q][0]
        if kind == 2:
            r = jnp.dot(permz_v[...], r.astype(BF), preferred_element_type=F32)
        for d in range(4):
            if kind == 1:
                block = jnp.concatenate([r[e * 96 + d * 24 : e * 96 + d * 24 + 24] for e in range(4)], axis=0)
            else:
                block = r[d * 96 : d * 96 + 96]
            target[d, :, col : col + n] = block.astype(BF)

    def weight_piece(q):
        group, _, taps = PIECES[q]
        for n, k in enumerate(taps):
            a = jnp.dot(hT[:, 0:ROWS], g5[:, k * C + group * WIDE : k * C + (group + 1) * WIDE], preferred_element_type=F32)
            b = jnp.dot(hT[:, ROWS:], g5p[:, k * WIDE : (k + 1) * WIDE], preferred_element_type=F32)
            store_first(q, a + b, n * WIDE, WIDE)
        if q == BIAS_PIECE:
            total = jnp.sum(bsum[...], axis=0, keepdims=True)
            total = jnp.broadcast_to(total, (128, C)).astype(BF)
            r = lax.dot_general(perm_v[0:HALF, :], total, NT, preferred_element_type=F32)
            store_first(q, r, WIDE, 128)
        send(q, 0)

    def weight_group(p):
        shift_g(gbuf, p, g5, lambda k: k * C + p * WIDE)
        g_copies[p].wait_recv()
        shift_g(gpar, p, g5p, lambda k: k * WIDE)
        for q, piece in enumerate(PIECES):
            if piece[0] == p:
                weight_piece(q)

    def arrived(q, stage, col, n):
        axis = ORDERS[PIECES[q][1]][stage]
        source, target = bufs[q][2 * stage], bufs[q][2 * stage + 1]
        total = source[pos[axis], :, col : col + n].astype(F32)
        for d in range(3):
            total = total + target[d, :, col : col + n].astype(F32)
        return total

    spread_row = lax.broadcasted_iota(jnp.int32, (64, 32), 0)
    spread_col = lax.broadcasted_iota(jnp.int32, (64, 32), 1)
    within = spread_row & 15
    spread = ((within < 6) & (spread_col == 6 * (spread_row >> 4) + within)).astype(F32).astype(BF)

    def finish(q, stage):
        for copy in hops[q, stage]:
            copy.wait_recv()
        group, _, taps = PIECES[q]
        for col in range(0, width(q), WIDE):
            n = min(WIDE, width(q) - col)
            total = arrived(q, stage, col, n)
            if stage == 0:
                for d in range(4):
                    block = jnp.concatenate([total[24 * d : 24 * d + 24], jnp.zeros((8, n), F32)], axis=0)
                    bufs[q][2][d, :, col : col + n] = block.astype(BF)
            elif stage == 1:
                r = jnp.dot(spread, total.astype(BF), preferred_element_type=F32).astype(BF)
                for d in range(4):
                    bufs[q][4][d, :, col : col + n] = r[16 * d : 16 * d + 16]
            elif n == WIDE:
                gws[taps[col // WIDE], :, group * WIDE : (group + 1) * WIDE] = total[0:8]
            else:
                gws[TAPS, :, 0:n] = total[0:8]
        if stage < 2:
            send(q, stage + 1)

    def finish_group(p, stage):
        for q, piece in enumerate(PIECES):
            if piece[0] == p:
                finish(q, stage)

    half = ROWS // 2

    def backward(t):
        base = t * half
        dhs[...] = sum(
            lax.dot_general(g5[base : base + half, k * C : (k + 1) * C], w_v[k * C : (k + 1) * C, :], NT, preferred_element_type=F32)
            for k in range(TAPS)
        )

        def tile(i, carry):
            row = pl.multiple_of(i * 32, 32)
            whole = pl.multiple_of(base + i * 32, 32)
            r = rin[pl.ds(whole, 32), 0:1]
            normed = xs[pl.ds(whole, 32), :] * r
            dn = dhs[pl.ds(row, 32), :] * gain[...]
            mean = jnp.mean(dn * normed, axis=-1, keepdims=True)
            g = cot_e[pl.ds(whole + HALO, 32), :].astype(F32) + (dn - normed * mean) * r
            gi[pl.ds(whole, 32), :] = g.astype(BF)
            return carry

        lax.fori_loop(0, half // 32, tile, 0)
        outgoing.append(local(gi.at[pl.ds(base, half)], gin.at[pl.ds(base, half)]))

    forward(0)
    forward(1)
    h_copy.wait_recv()
    weight_group(0)
    forward(2)
    finish_group(0, 0)
    weight_group(1)
    finish_group(0, 1)
    finish_group(1, 0)
    weight_group(2)
    finish_group(0, 2)
    finish_group(1, 1)
    backward(0)
    finish_group(2, 0)
    finish_group(1, 2)
    backward(1)
    finish_group(2, 1)
    finish_group(2, 2)

    gw[...] = gws[0:TAPS, 0:6, :]
    mine = (dp * 8 + seq) * 6
    base = jnp.minimum(lax.div(mine, 16) * 16, C - 32)
    pick_row = lax.broadcasted_iota(jnp.int32, (8, 32), 0)
    pick_col = lax.broadcasted_iota(jnp.int32, (8, 32), 1)
    pick = (pick_col == pick_row + (mine - base)).astype(F32).astype(BF)
    total = jnp.zeros((8, C), F32)
    for k in range(TAPS):
        rows = w_v[pl.ds(pl.multiple_of(k * C + base, 16), 32), :]
        total = total + jnp.dot(pick, rows, preferred_element_type=F32) * gws[k]
    lane = lax.broadcasted_iota(jnp.int32, (8, C), 1)
    row = lax.broadcasted_iota(jnp.int32, (8, C), 0)
    own_gain = jnp.sum(jnp.where(lane == row + mine, gain[...], 0.0), axis=-1, keepdims=True)
    column = jnp.sum(total, axis=-1, keepdims=True) / own_gain
    diagonal = (lane == row)[:, 0:128] & (row < 6)[:, 0:128]
    ggain[...] = jnp.sum(jnp.where(diagonal, column, 0.0), axis=0, keepdims=True)[:, 0:6]
    gbias[...] = jnp.sum(jnp.where(diagonal, gws[TAPS, :, 0:128], 0.0), axis=0, keepdims=True)[:, 0:6]

    for copy in outgoing:
        copy.wait()
    for copy in started:
        copy.wait_send()


MESH = pl.DeviceIdType.MESH


def body(bases, upsampled, base_table, filter_weight, filter_bias, norm_gain, cotangent):
    perm, perm_z = permutations()
    vmem, hbm = pl.BlockSpec(memory_space=pltpu.VMEM), pl.BlockSpec(memory_space=pl.ANY)
    scratch = [
        pltpu.VMEM((1, ROWS + 256), jnp.int32),
        pltpu.VMEM((EXT, C), BF),
        pltpu.VMEM((EXT, C), BF),
        pltpu.VMEM((TAPS * C, C), BF),
        pltpu.VMEM((C, C), BF),
        pltpu.VMEM((HALF, HALF), BF),
        pltpu.VMEM((8, C), F32),
        pltpu.VMEM((ROWS, C), F32),
        pltpu.VMEM((ROWS, 128), F32),
        pltpu.VMEM((EXT + 2 * HALO, C), BF),
        pltpu.VMEM((EXT, TAPS * C), BF),
        pltpu.VMEM((HALF, 2 * ROWS), BF),
        pltpu.VMEM((HALF, ROWS), BF),
        pltpu.VMEM((EXT, WIDE), F32),
        pltpu.VMEM((GROUPS, EXT, WIDE), BF),
        pltpu.VMEM((GROUPS, EXT, WIDE), BF),
        pltpu.VMEM((ROWS, TAPS * C), BF),
        pltpu.VMEM((ROWS, TAPS * WIDE), BF),
        pltpu.VMEM((8, C), F32),
        pltpu.VMEM((ROWS, C), BF),
        pltpu.VMEM((ROWS, C), BF),
        pltpu.VMEM((ROWS // 2, C), F32),
        pltpu.VMEM((TAPS + 1, 8, C), F32),
    ]
    for q in range(len(PIECES)):
        for rows in (96, 32, 16):
            scratch += [pltpu.VMEM((4, rows, width(q)), BF), pltpu.VMEM((3, rows, width(q)), BF)]
    remotes = 6 + 1 + GROUPS + 9 * len(PIECES)
    scratch += [
        pltpu.SemaphoreType.DMA((16,)),
        pltpu.SemaphoreType.DMA((remotes,)),
        pltpu.SemaphoreType.DMA((remotes,)),
    ]
    out, gin, gw, gbias, ggain = pl.pallas_call(
        kernel,
        out_shape=[
            jax.ShapeDtypeStruct((ROWS, C), BF),
            jax.ShapeDtypeStruct((ROWS, C), BF),
            jax.ShapeDtypeStruct((TAPS, 6, C), F32),
            jax.ShapeDtypeStruct((1, 6), F32),
            jax.ShapeDtypeStruct((1, 6), F32),
        ],
        in_specs=[hbm, hbm, vmem, hbm, vmem, vmem, hbm, hbm, hbm],
        out_specs=[hbm, hbm, vmem, vmem, vmem],
        scratch_shapes=scratch,
        compiler_params=pltpu.CompilerParams(collective_id=0, has_side_effects=True, vmem_limit_bytes=62 * 2**20),
        name="block",
    )(
        bases,
        upsampled[0],
        base_table,
        filter_weight.reshape(TAPS * C, C),
        filter_bias[None],
        norm_gain[None],
        cotangent[0],
        jnp.asarray(perm, BF),
        jnp.asarray(perm_z, BF),
    )
    return out[None], gin[None], gw, gbias[0], ggain[0]


def solution(mesh):
    placed = (P("dp", "seq"), P("dp", "seq", None), P(), P(), P(), P(), P("dp", "seq", None))
    return jax.shard_map(
        body,
        mesh=mesh,
        in_specs=placed,
        out_specs=(
            P("dp", "seq", None),
            P("dp", "seq", None),
            P(None, ("dp", "seq"), None),
            P(("dp", "seq")),
            P(("dp", "seq")),
        ),
        check_vma=False,
    )
```

time: 223 us -> 81.6 us (0.37)
  waiting for transfers between devices: 76.3 us -> 0 us
  Pallas kernels: 0 us -> 72.6 us
  blocking collectives: 68.2 us -> 0 us
  matrix products: 40.7 us -> 0 us
  between operations: 14.3 us -> 0.66 us
  starting transfers between devices: 12 us -> 0 us
  other arithmetic: 5.92 us -> 0 us
  local copies, waits for them, and re-layouts: 4.19 us -> 8.14 us
    unnamed x2 -> x0, waiting for transfers between devices: 76.3 us -> none
    pallas_call x0 -> x1, Pallas kernels: none -> 72.6 us  [body(): pl.pallas_call(kernel, out_shape=[jax.ShapeDtypeStruct((ROWS, C), BF), ja...]
    unnamed x1 -> x0, blocking collectives: 68.2 us -> none
    dot_general x16 -> x0, matrix products: 40.7 us -> none  [the longest x5 14.4 us: body(): jnp.einsum('as,af->sf', padded_input[tap_index * DILATION_STEP:tap_index...]
    ppermute x4 -> x0, starting transfers between devices: 12 us -> none  [the longest x2 9.3 us: extended(): lax.ppermute(tail, axis, [(i, (i + 1) % count) for i in range(ends)])]
    broadcast_in_dim x1 -> x0, other arithmetic: 5.54 us -> none  [body(): grad_in.astype(jnp.bfloat16)[None]]
    broadcast_in_dim x0 -> x2, local copies, waits for them, and re-layouts: none -> 2.53 us  [the longest x1 1.27 us: body(): filter_bias[None]]
    unnamed x23 -> x13, local copies, waits for them, and re-layouts: 3.45 us -> 5.6 us
  transfers between devices with their start and end apart: 5 -> 0, of which waited for: 1 -> 0; matrix products, arithmetic and copies ran while one was open for 11% -> 0% of each run, Pallas kernels for 0% -> 0%
where the time goes in v1:
time: 81.6 us; the launch traced here: 81.4 us
  Pallas kernels  72.6 us (89%)
  local copies, waits for them, and re-layouts  8.14 us (10%)
    pallas_call x1, Pallas kernels, body(): pl.pallas_call(kernel, out_shape=[jax.ShapeDtypeStruct((ROWS, C), BF), ja...  72.6 us
    unnamed x13, local copies, waits for them, and re-layouts  5.6 us

profile of v1, /device:TPU:0, one launch (start us, length us, event | category | flops | bytes accessed | tf_op | source)
XLA Modules:
  0.0 81.4 jit_solution(13994723922129002532)
XLA Ops:
  0.6 1.3 %broadcast_in_dim.12.refs_4_ = f32[1,768]{1,0:T(1,128)} reshape(f32[768]{0:T(1024)} %param.13) | data formatting | bytes 6144 | tf_op jit(solution)/shard_map/broadcast_in_dim | solution.py:434
  1.9 1.3 %broadcast_in_dim.13.refs_5_ = f32[1,768]{1,0:T(1,128)} reshape(f32[768]{0:T(1024)} %param.14) | data formatting | bytes 6144 | tf_op jit(solution)/shard_map/broadcast_in_dim | solution.py:435
  3.2 72.6 %block.1 = (bf16[1024,768]{1,0:T(8,128)(2,1)}, bf16[1024,768]{1,0:T(8,128)(2,1)}, f32[5,6,768]{2,1,0:T(8,128)}, f32[1,6]{1,0:T(1,128)}, f32[1,6]{1,0:T(1,128)}) custom-call(s32[1,1024]{1,0:T(1,128)} %refs_0_.1, bf16[1024,768]{1,0:T(8,128)(2,1)} %bitcast.8, bf16[4,768]{1,0:T(4,128)(2,1)} %refs_2_.1, bf16[3840,768]{1,0:T(8,128)(2,1)} %bitcast.7, ...), custom_call_target="tpu_custom_call" | custom-call | tf_op jit(solution)/shard_map/block/pallas_call | solution.py:415
  75.7 0.0 copy-start
  75.7 2.8 %copy.19 = bf16[1,1024,768]{2,1,0:T(8,128)(2,1)} copy(bf16[1,1024,768]{2,1,0:T(8,128)(2,1)} %bitcast.11) | data formatting | bytes 3145728
  78.5 0.0 copy-done
  78.5 0.0 copy-start.1
  78.5 0.0 copy-start.3
  78.5 0.0 copy-start.2
  78.5 1.1 %copy.20 = bf16[1,1024,768]{2,1,0:T(8,128)(2,1)} copy(bf16[1,1024,768]{2,1,0:T(8,128)(2,1)S(1)} %bitcast.10) | data formatting | bytes 3145728
  79.7 0.0 copy-done.1
  79.7 0.6 copy.21
  80.3 0.0 copy-done.3
  80.3 0.5 copy.22
  80.8 0.0 copy-done.2
  80.8 0.5 copy.23
Async XLA Ops:
  75.7 2.8 %copy-start = (bf16[1024,768]{1,0:T(8,128)(2,1)S(1)}, bf16[1024,768]{1,0:T(8,128)(2,1)}, u32[]{:S(2)}) copy-start(bf16[1024,768]{1,0:T(8,128)(2,1)} %get-tuple-element.11) | copy-start | bytes 4718596
  78.5 1.2 %copy-start.1 = (f32[5,6,768]{2,1,0:T(8,128)S(1)}, f32[5,6,768]{2,1,0:T(8,128)}, u32[]{:S(2)}) copy-start(f32[5,6,768]{2,1,0:T(8,128)} %get-tuple-element.22) | copy-start | bytes 276484
  78.5 1.8 %copy-start.3 = (f32[1,6]{1,0:T(1,128)S(1)}, f32[1,6]{1,0:T(1,128)}, u32[]{:S(2)}) copy-start(f32[1,6]{1,0:T(1,128)} %get-tuple-element.13) | copy-start | bytes 76
  78.5 2.3 %copy-start.2 = (f32[1,6]{1,0:T(1,128)S(1)}, f32[1,6]{1,0:T(1,128)}, u32[]{:S(2)}) copy-start(f32[1,6]{1,0:T(1,128)} %get-tuple-element.14) | copy-start | bytes 76

commit v2 on v1

v2 whole, which is shorter than its diff:
```python
import jax
import jax.numpy as jnp
import numpy as np
from jax import lax
from jax.experimental import pallas as pl
from jax.experimental.pallas import tpu as pltpu
from jax.sharding import PartitionSpec as P

BF, F32 = jnp.bfloat16, jnp.float32
C, TAPS, STEP = 768, 5, 4
ROWS, HALO = 1024, 16
EXT = ROWS + 2 * HALO
WIDE = 256
GROUPS = C // WIDE
HALF = C // 2
NT = (((1,), (1,)), ((), ()))
TN = (((0,), (0,)), ((), ()))

TAP_OF = [3 * slot % TAPS for slot in range(TAPS)]
SLOTS = ((0, 2), (2, 2), (4, 1))
STAGES = 3
TILE = 256
BLOCK_ROWS = (96, 32, 16)


def here():
    dp, seq = lax.axis_index("dp"), lax.axis_index("seq")
    x = 2 * lax.div(dp, 8) + lax.rem(seq, 2)
    return [x, lax.rem(lax.div(dp, 2), 4), lax.div(seq, 2)], lax.rem(dp, 2), dp, seq


def place(pos, core):
    x, y, z = pos
    return (lax.div(x, 2) * 8 + y * 2 + core, z * 2 + lax.rem(x, 2))


def moved(pos, axis, delta):
    other = list(pos)
    other[axis] = lax.rem(pos[axis] + delta, 4)
    return other


def times(value, step):
    return pl.multiple_of(value * step, step)


def kernel(*refs):
    names = iter(refs)

    def take(n):
        return [next(names) for _ in range(n)]

    bases, up, table, weight, bias_in, gain_in, cot = take(7)
    ob, gi, gw, small = take(4)
    bases_e, up_e, cot_e, w_v, perm_v, permz_v, tab, xs, rin, hb, h5, hs, h_in, pre = take(14)
    gbuf, gpar, g5, g5p, bsum, dh_a, dh_b, gws, bias, gain = take(10)
    blocks, others, bias_blocks, bias_others = take(3), take(3), take(3), take(3)
    wres = next(names)
    local_sem, send_sem, recv_sem = take(3)

    pos, core, dp, seq = here()
    partner = place(pos, 1 - core)
    left, right = (dp, lax.rem(seq + 7, 8)), (dp, lax.rem(seq + 1, 8))
    inside = (seq > 0, seq < 7)

    def remote(n, src, dst, device):
        return pltpu.make_async_remote_copy(
            src_ref=src, dst_ref=dst, send_sem=send_sem.at[n], recv_sem=recv_sem.at[n],
            device_id=device, device_id_type=MESH,
        )

    def local(n, src, dst):
        return pltpu.make_async_copy(src, dst, local_sem.at[n])

    in_bases = local(0, bases, bases_e.at[:, pl.ds(128, ROWS)])
    in_up = local(1, up, up_e.at[pl.ds(HALO, ROWS)])
    in_row = [local(2, bias_in, bias.at[0]), local(3, gain_in, gain.at[0])]
    in_w = [local(6 + p, weight.at[:, pl.ds(p * WIDE, WIDE)], w_v.at[:, pl.ds(p * WIDE, WIDE)]) for p in range(GROUPS)]
    in_cot = local(9, cot, cot_e.at[pl.ds(HALO, ROWS)])
    for copy in (in_bases, in_up, *in_row, *in_w, in_cot):
        copy.start()

    barrier = pltpu.get_barrier_semaphore()
    partners = [partner, left, right]
    partners += [place(moved(pos, axis, delta), core) for axis in range(3) for delta in (1, 2, 3)]
    for device in partners:
        pl.semaphore_signal(barrier, inc=1, device_id=device, device_id_type=MESH)

    halos = [
        remote(0, bases.at[:, pl.ds(ROWS - 128, 128)], bases_e.at[:, pl.ds(0, 128)], right),
        remote(1, bases.at[:, pl.ds(0, 128)], bases_e.at[:, pl.ds(128 + ROWS, 128)], left),
    ]
    for n, (source, target) in enumerate(((up, up_e), (cot, cot_e))):
        halos += [
            remote(2 + 2 * n, source.at[pl.ds(ROWS - HALO, HALO)], target.at[pl.ds(0, HALO)], right),
            remote(3 + 2 * n, source.at[pl.ds(0, HALO)], target.at[pl.ds(HALO + ROWS, HALO)], left),
        ]
    h_copy = remote(6, hs.at[1], h_in, partner)

    def g_copy(p):
        return remote(7 + p, gbuf.at[p], gpar.at[p], partner)

    row = lax.broadcasted_iota(jnp.int32, (HALF, 128), 0)
    column = lax.broadcasted_iota(jnp.int32, (HALF, 128), 1)
    sixth = (row * 10923) >> 16
    last = row - 6 * sixth
    first, second, third = sixth >> 4, (sixth >> 2) & 3, sixth & 3
    channel = (first >> 1) * 384 + second * 96 + third * 12 + (first & 1) * 6 + last
    for n, c in enumerate((core, 1 - core)):
        for b in range(C // 128):
            hit = column + b * 128 == channel + c * 48
            perm_v[n * HALF : (n + 1) * HALF, b * 128 : (b + 1) * 128] = hit.astype(F32).astype(BF)
    kept = second * 96 + third * 24 + first * 6 + last
    for b in range(HALF // 128):
        permz_v[:, b * 128 : (b + 1) * 128] = (column + b * 128 == kept).astype(F32).astype(BF)

    tab[...] = jnp.zeros(tab.shape, F32)
    tab[0:4, :] = table[...].astype(F32)
    bsum[...] = jnp.zeros(bsum.shape, F32)
    code = lax.broadcasted_iota(jnp.int32, (8, 128), 0)

    def embedded(block):
        onehot = (code == bases_e[:, pl.ds(times(block, 128), 128)]).astype(F32)
        return lax.dot_general(onehot, tab[...], TN, preferred_element_type=F32)

    def normed_of(x):
        r = lax.rsqrt(jnp.mean(x * x, axis=-1, keepdims=True) + 1e-06)
        return r, (x * r * gain[...])

    def norm_block(b, carry):
        e = embedded(b + 1)
        for s in range(4):
            row = pl.multiple_of(b * 128 + s * 32, 32)
            x = up_e[pl.ds(row + HALO, 32), :].astype(F32) + e[s * 32 : s * 32 + 32]
            r, h = normed_of(x)
            xs[pl.ds(row, 32), :] = x
            rin[pl.ds(row, 32), :] = jnp.broadcast_to(r, (32, 128))
            hb[pl.ds(row + 2 * HALO, 32), :] = h.astype(BF)
        return carry

    def norm():
        for copy in (in_bases, in_up, *in_row):
            copy.wait()
        lax.fori_loop(0, ROWS // 128, norm_block, 0)
        pl.semaphore_wait(barrier, len(partners))
        for copy in halos:
            copy.start()

    def norm_ends():
        for copy in halos:
            copy.wait_recv()
        hb[0:HALO, :] = jnp.zeros((HALO, C), BF)
        hb[HALO + EXT : 2 * HALO + EXT, :] = jnp.zeros((HALO, C), BF)
        for side, (block, skip) in enumerate(((0, 128 - HALO), (1 + ROWS // 128, 0))):
            start = side * (HALO + ROWS)
            x = up_e[start : start + HALO, :].astype(F32) + embedded(block)[skip : skip + HALO]
            h = jnp.where(inside[side], normed_of(x)[1], 0.0)
            hb[start + HALO : start + 2 * HALO, :] = h.astype(BF)

    def turn():
        def one(n, carry):
            rows = perm_v[pl.ds(times(1 - n, HALF), HALF), :]
            h_own = hb[2 * HALO : 2 * HALO + ROWS, :]
            hs[1 - n] = lax.dot_general(rows, h_own, NT, preferred_element_type=F32).astype(BF)
            pl.when(n == 0)(h_copy.start)
            return carry

        lax.fori_loop(0, 2, one, 0)

    def shift_h():
        def tile(j, carry):
            row = times(j, 96)
            for p in range(GROUPS):
                v = hb[pl.ds(row, 128), p * WIDE : (p + 1) * WIDE].astype(F32)
                for k in range(TAPS):
                    h5[pl.ds(row, 96), k * C + p * WIDE : k * C + (p + 1) * WIDE] = v[8 + STEP * k : 104 + STEP * k].astype(BF)
            return carry

        lax.fori_loop(0, EXT // 96, tile, 0)

    c0 = np.float32(np.sqrt(2 / np.pi))

    def gelu_pair(z):
        square = z * z
        t = jnp.tanh(c0 * z * (1 + 0.044715 * square))
        cdf = 0.5 + 0.5 * t
        slope = cdf + (0.5 * c0) * z * (1 - t * t) * (1 + 0.134145 * square)
        return z * cdf, slope

    def forward(p):
        cols = pl.ds(times(p, WIDE), WIDE)
        for n in range(GROUPS):
            pl.when(p == n)(in_w[n].wait)
        pl.when(p == 0)(in_cot.wait)
        pre[...] = jnp.dot(h5[...], w_v[:, cols], preferred_element_type=F32)

        def tile(i, carry):
            row = times(i, 64)
            act, slope = gelu_pair(pre[pl.ds(row + HALO, 64), :] + bias[:, cols])
            ob[pl.ds(row, 64), cols] = (xs[pl.ds(row, 64), cols] + act).astype(BF)
            gbuf[p, pl.ds(row + HALO, 64), :] = (cot_e[pl.ds(row + HALO, 64), cols].astype(F32) * slope).astype(BF)
            return carry

        lax.fori_loop(0, ROWS // 64, tile, 0)
        for side in range(2):
            rows = slice(side * (HALO + ROWS), side * (HALO + ROWS) + HALO)
            _, slope = gelu_pair(pre[rows, :] + bias[:, cols])
            g = jnp.where(inside[side], cot_e[rows, cols].astype(F32) * slope, 0.0)
            gbuf[p, rows, :] = g.astype(BF)
        g_copy(p).start()

    def shift_g(source, p, target, column):
        def tile(j, total):
            row = times(j, 128)
            v = source[p, pl.ds(row, 160), :].astype(F32)
            for k in range(TAPS):
                target[pl.ds(row, 128), pl.ds(column(k), WIDE)] = v[24 - STEP * k : 152 - STEP * k].astype(BF)
            return total + jnp.sum(v[16:144].reshape(16, 8, WIDE), axis=0)

        bsum[:, pl.ds(times(p, WIDE), WIDE)] += lax.fori_loop(0, ROWS // 128, tile, jnp.zeros((8, WIDE), F32))

    def axis_of(kind, stage):
        return (kind, jnp.where(kind == 0, 1, 0), jnp.where(kind == 2, 1, 2))[stage]

    def along(axis):
        return jnp.where(axis == 0, pos[0], jnp.where(axis == 1, pos[1], pos[2]))

    def hops(first, axis, source, target):
        copies = []
        for delta in (1, 2, 3):
            other = [lax.rem(pos[a] + jnp.where(axis == a, delta, 0), 4) for a in range(3)]
            copies.append(remote(first + delta - 1, source(along(axis) + delta), target(delta - 1), place(other, core)))
        return copies

    def piece_hops(p, m, stage):
        slot, count = SLOTS[m]
        axis = axis_of(lax.rem(p + m, 3), stage)
        return hops(
            10 + ((p * 3 + m) * STAGES + stage) * 3,
            axis,
            lambda d: blocks[stage].at[p, lax.rem(d, 4), pl.ds(slot, count)],
            lambda d: others[stage].at[p, d, pl.ds(slot, count)],
        )

    def bias_hops(stage):
        return hops(
            10 + 27 * GROUPS + stage * 3,
            jnp.int32(stage),
            lambda d: bias_blocks[stage].at[lax.rem(d, 4)],
            lambda d: bias_others[stage].at[d],
        )

    def weights(p):
        shift_g(gbuf, p, g5, lambda k: pl.multiple_of(k * C + p * WIDE, WIDE))
        g_copy(p).wait_recv()
        shift_g(gpar, p, g5p, lambda k: TAP_OF.index(k) * WIDE)

        @pl.when(p == 0)
        def _():
            h_copy.wait_recv()

        def piece(m, first, count):
            own = [g5[:, pl.ds(pl.multiple_of(lax.rem(3 * (first + n), TAPS) * C + p * WIDE, WIDE), WIDE)] for n in range(count)]
            other = g5p[:, pl.ds(times(first, WIDE), count * WIDE)]
            rhs = jnp.concatenate([jnp.concatenate(own, axis=1) if count > 1 else own[0], other], axis=0)
            lhs = jnp.concatenate([hs[0], h_in[...]], axis=1)
            wres[:, 0 : count * WIDE] = jnp.dot(lhs, rhs, preferred_element_type=F32)
            kind = lax.rem(p + m, 3)
            for n in range(count):
                cols = slice(n * WIDE, (n + 1) * WIDE)

                def store(block):
                    for d in range(4):
                        blocks[0][p, d, first + n] = block(d).astype(BF)

                @pl.when(kind == 0)
                def _():
                    store(lambda d: wres[d * 96 : d * 96 + 96, cols])

                @pl.when(kind == 1)
                def _():
                    store(lambda d: jnp.concatenate([wres[e * 96 + d * 24 : e * 96 + d * 24 + 24, cols] for e in range(4)], axis=0))

                @pl.when(kind == 2)
                def _():
                    r = jnp.dot(permz_v[...], wres[:, cols].astype(BF), preferred_element_type=F32)
                    store(lambda d: r[d * 96 : d * 96 + 96])

        def pair(m, carry):
            piece(m, 2 * m, 2)
            for n in range(2):

                @pl.when(m == n)
                def _():
                    for copy in piece_hops(p, n, 0):
                        copy.start()

            return carry

        lax.fori_loop(0, 2, pair, 0)
        piece(2, 4, 1)
        for copy in piece_hops(p, 2, 0):
            copy.start()

        @pl.when(p == GROUPS - 1)
        def _():
            total = jnp.sum(bsum[...], axis=0, keepdims=True)
            total = jnp.broadcast_to(total, (128, C)).astype(BF)
            r = lax.dot_general(perm_v[0:HALF, :], total, NT, preferred_element_type=F32)
            for d in range(4):
                bias_blocks[0][d] = r[d * 96 : d * 96 + 96].astype(BF)
            for copy in bias_hops(0):
                copy.start()

    spread_row = lax.broadcasted_iota(jnp.int32, (64, 32), 0)
    spread_col = lax.broadcasted_iota(jnp.int32, (64, 32), 1)
    within = spread_row & 15
    spread = ((within < 6) & (spread_col == 6 * (spread_row >> 4) + within)).astype(F32).astype(BF)

    def handed_on(total, stage, store):
        if stage == 0:
            for d in range(4):
                block = jnp.concatenate([total[24 * d : 24 * d + 24], jnp.zeros((8, total.shape[1]), F32)], axis=0)
                store(d, block.astype(BF))
        else:
            r = jnp.dot(spread, total.astype(BF), preferred_element_type=F32).astype(BF)
            for d in range(4):
                store(d, r[16 * d : 16 * d + 16])

    def finish(p, stage):
        for m, (first, count) in enumerate(SLOTS):
            for copy in piece_hops(p, m, stage):
                copy.wait_recv()
            own = along(axis_of(lax.rem(p + m, 3), stage))
            for slot in range(first, first + count):
                total = blocks[stage][p, own, slot].astype(F32)
                for d in range(3):
                    total = total + others[stage][p, d, slot].astype(F32)
                if stage == 2:
                    gws[TAP_OF[slot], :, pl.ds(times(p, WIDE), WIDE)] = total[0:8]
                else:

                    def store(d, value):
                        blocks[stage + 1][p, d, slot] = value

                    handed_on(total, stage, store)
            if stage < 2:
                for copy in piece_hops(p, m, stage + 1):
                    copy.start()

    def finish_bias(stage):
        for copy in bias_hops(stage):
            copy.wait_recv()
        total = bias_blocks[stage][pos[stage]].astype(F32)
        for d in range(3):
            total = total + bias_others[stage][d].astype(F32)
        if stage == 2:
            gws[TAPS, :, 0:128] = total[0:8]
        else:

            def store(d, value):
                bias_blocks[stage + 1][d] = value

            handed_on(total, stage, store)
            for copy in bias_hops(stage + 1):
                copy.start()

    def hidden(t):
        rows = pl.ds(times(t, TILE), TILE)
        return sum(
            lax.dot_general(g5[rows, k * C : (k + 1) * C], w_v[k * C : (k + 1) * C, :], NT, preferred_element_type=F32)
            for k in range(TAPS)
        )

    def input_gradient(t, dh):
        for i in range(TILE // 32):
            row = pl.multiple_of(t * TILE + i * 32, 32)
            r = jnp.concatenate([rin[pl.ds(row, 32), :]] * (C // 128), axis=1)
            normed = xs[pl.ds(row, 32), :] * r
            dn = dh[i * 32 : i * 32 + 32, :] * gain[...]
            mean = jnp.mean(dn * normed, axis=-1, keepdims=True)
            g = cot_e[pl.ds(row + HALO, 32), :].astype(F32) + (dn - normed * mean) * r
            gi[pl.ds(row, 32), :] = g.astype(BF)

    def backward(u):
        dh_a[...] = hidden(2 * u)
        input_gradient(jnp.maximum(2 * u - 1, 0), dh_b)
        dh_b[...] = hidden(2 * u + 1)
        input_gradient(2 * u, dh_a)

    def during(s, start, stop, step):
        if stop > start:
            pl.when((s >= start) & (s < stop))(step)

    def turn_of(s, carry):
        during(s, 0, 3, lambda: forward(s))
        during(s, 1, 4, lambda: weights(s - 1))
        during(s, 4, 6, lambda: backward(s - 4))
        for stage in range(STAGES):
            during(s, 2 + stage, 5 + stage, lambda: finish(s - 2 - stage, stage))
            during(s, 4 + stage, 5 + stage, lambda: finish_bias(stage))
        return carry

    norm()
    turn()
    norm_ends()
    shift_h()
    dh_b[...] = jnp.zeros(dh_b.shape, F32)
    lax.fori_loop(0, 6, turn_of, 0)
    input_gradient(ROWS // TILE - 1, dh_b)
    finish(2, 2)
    finish_bias(2)

    gw[...] = gws[0:TAPS, 0:6, :]
    mine = (dp * 8 + seq) * 6
    base = jnp.minimum(lax.div(mine, 16) * 16, C - 32)
    pick_row = lax.broadcasted_iota(jnp.int32, (8, 32), 0)
    pick_col = lax.broadcasted_iota(jnp.int32, (8, 32), 1)
    pick = (pick_col == pick_row + (mine - base)).astype(F32).astype(BF)
    total = jnp.zeros((8, C), F32)
    for k in range(TAPS):
        rows = w_v[pl.ds(pl.multiple_of(k * C + base, 16), 32), :]
        total = total + jnp.dot(pick, rows, preferred_element_type=F32) * gws[k]
    lane = lax.broadcasted_iota(jnp.int32, (8, C), 1)
    row = lax.broadcasted_iota(jnp.int32, (8, C), 0)
    own_gain = jnp.sum(jnp.where(lane == row + mine, gain[...], 0.0), axis=-1, keepdims=True)
    column = jnp.sum(total, axis=-1, keepdims=True) / own_gain
    diagonal = (lane == row)[:, 0:128] & (row < 6)[:, 0:128]
    small[0:1, :] = jnp.sum(jnp.where(diagonal, gws[TAPS, :, 0:128], 0.0), axis=0, keepdims=True)
    small[1:2, :] = jnp.sum(jnp.where(diagonal, column, 0.0), axis=0, keepdims=True)

    for copy in (*halos, h_copy):
        copy.wait_send()
    for stage in range(STAGES):
        for copy in bias_hops(stage):
            copy.wait_send()

    def sent(p, carry):
        g_copy(p).wait_send()
        for m in range(3):
            for stage in range(STAGES):
                for copy in piece_hops(p, m, stage):
                    copy.wait_send()
        return carry

    lax.fori_loop(0, GROUPS, sent, 0)


MESH = pl.DeviceIdType.MESH


def body(bases, upsampled, base_table, filter_weight, filter_bias, norm_gain, cotangent):
    vmem, hbm = pl.BlockSpec(memory_space=pltpu.VMEM), pl.BlockSpec(memory_space=pl.ANY)
    scratch = [
        pltpu.VMEM((1, ROWS + 256), jnp.int32),
        pltpu.VMEM((EXT, C), BF),
        pltpu.VMEM((EXT, C), BF),
        pltpu.VMEM((TAPS * C, C), BF),
        pltpu.VMEM((C, C), BF),
        pltpu.VMEM((HALF, HALF), BF),
        pltpu.VMEM((8, C), F32),
        pltpu.VMEM((ROWS, C), F32),
        pltpu.VMEM((ROWS, 128), F32),
        pltpu.VMEM((EXT + 2 * HALO, C), BF),
        pltpu.VMEM((EXT, TAPS * C), BF),
        pltpu.VMEM((2, HALF, ROWS), BF),
        pltpu.VMEM((HALF, ROWS), BF),
        pltpu.VMEM((EXT, WIDE), F32),
        pltpu.VMEM((GROUPS, EXT, WIDE), BF),
        pltpu.VMEM((GROUPS, EXT, WIDE), BF),
        pltpu.VMEM((ROWS, TAPS * C), BF),
        pltpu.VMEM((ROWS, TAPS * WIDE), BF),
        pltpu.VMEM((8, C), F32),
        pltpu.VMEM((TILE, C), F32),
        pltpu.VMEM((TILE, C), F32),
        pltpu.VMEM((TAPS + 1, 8, C), F32),
        pltpu.VMEM((1, C), F32),
        pltpu.VMEM((1, C), F32),
    ]
    scratch += [pltpu.VMEM((GROUPS, 4, TAPS, rows, WIDE), BF) for rows in BLOCK_ROWS]
    scratch += [pltpu.VMEM((GROUPS, 3, TAPS, rows, WIDE), BF) for rows in BLOCK_ROWS]
    scratch += [pltpu.VMEM((4, rows, 128), BF) for rows in BLOCK_ROWS]
    scratch += [pltpu.VMEM((3, rows, 128), BF) for rows in BLOCK_ROWS]
    scratch += [pltpu.VMEM((HALF, 2 * WIDE), F32)]
    remotes = 10 + 27 * GROUPS + 9
    scratch += [
        pltpu.SemaphoreType.DMA((16,)),
        pltpu.SemaphoreType.DMA((remotes,)),
        pltpu.SemaphoreType.DMA((remotes,)),
    ]
    out, gin, gw, small = pl.pallas_call(
        kernel,
        out_shape=[
            pltpu.VMEM((ROWS, C), BF),
            pltpu.VMEM((ROWS, C), BF),
            pltpu.VMEM((TAPS, 6, C), F32),
            pltpu.VMEM((8, 128), F32),
        ],
        in_specs=[hbm, hbm, vmem, hbm, hbm, hbm, hbm],
        out_specs=[vmem, vmem, vmem, vmem],
        scratch_shapes=scratch,
        compiler_params=pltpu.CompilerParams(collective_id=0, has_side_effects=True, vmem_limit_bytes=58 * 2**20),
        name="block",
    )(
        bases,
        upsampled[0],
        base_table,
        filter_weight.reshape(TAPS * C, C),
        filter_bias,
        norm_gain,
        cotangent[0],
    )
    return out[None], gin[None], gw, small[0, 0:6], small[1, 0:6]


def solution(mesh):
    placed = (P("dp", "seq"), P("dp", "seq", None), P(), P(), P(), P(), P("dp", "seq", None))
    return jax.shard_map(
        body,
        mesh=mesh,
        in_specs=placed,
        out_specs=(
            P("dp", "seq", None),
            P("dp", "seq", None),
            P(None, ("dp", "seq"), None),
            P(("dp", "seq")),
            P(("dp", "seq")),
        ),
        check_vma=False,
    )
```

time: 81.6 us -> 63.3 us (0.78)
  Pallas kernels: 72.6 us -> 59.1 us
  local copies, waits for them, and re-layouts: 8.14 us -> 3.45 us
    pallas_call x1, Pallas kernels: 72.6 us -> 59.1 us  [body(): pl.pallas_call(kernel, out_shape=[pltpu.VMEM((ROWS, C), BF), pltpu.VMEM((...]
    unnamed x13 -> x3, local copies, waits for them, and re-layouts: 5.6 us -> 2.93 us
    broadcast_in_dim x2 -> x0, local copies, waits for them, and re-layouts: 2.53 us -> none  [the longest x1 1.27 us: body(): filter_bias[None]]
where the time goes in v2:
time: 63.3 us; the launch traced here: 63.2 us
  Pallas kernels  59.1 us (93%)
  local copies, waits for them, and re-layouts  3.45 us (5%)
  between operations  0.64 us (1%)
    pallas_call x1, Pallas kernels, body(): pl.pallas_call(kernel, out_shape=[pltpu.VMEM((ROWS, C), BF), pltpu.VMEM((...  59.1 us
    unnamed x3, local copies, waits for them, and re-layouts  2.93 us

profile of v2, /device:TPU:0, one launch (start us, length us, event | category | flops | bytes accessed | tf_op | source)
XLA Modules:
  0.0 63.2 jit_solution(496937634072863822)
XLA Ops:
  0.6 59.1 %block.1 = (bf16[1024,768]{1,0:T(8,128)(2,1)S(1)}, bf16[1024,768]{1,0:T(8,128)(2,1)S(1)}, f32[5,6,768]{2,1,0:T(8,128)S(1)}, f32[8,128]{1,0:T(8,128)S(1)}) custom-call(s32[1,1024]{1,0:T(1,128)} %refs_0_.1, bf16[1024,768]{1,0:T(8,128)(2,1)} %bitcast.12, bf16[4,768]{1,0:T(4,128)(2,1)} %refs_2_.1, bf16[3840,768]{1,0:T(8,128)(2,1)} %bitcast.11, f32[768]{0:T(1024)} %refs_4_.1, ...), custom_call_target="tpu_custom_call" | custom-call | tf_op jit(solution)/shard_map/block/pallas_call | solution.py:491
  59.7 0.5 slice_bitcast_fusion
  60.2 1.1 %copy.15 = bf16[1,1024,768]{2,1,0:T(8,128)(2,1)} copy(bf16[1,1024,768]{2,1,0:T(8,128)(2,1)S(1)} %bitcast.10) | data formatting | bytes 3145728
  61.4 1.1 %copy.16 = bf16[1,1024,768]{2,1,0:T(8,128)(2,1)} copy(bf16[1,1024,768]{2,1,0:T(8,128)(2,1)S(1)} %bitcast.9) | data formatting | bytes 3145728
  62.5 0.6 %copy.17 = f32[5,6,768]{2,1,0:T(8,128)} copy(f32[5,6,768]{2,1,0:T(8,128)S(1)} %get-tuple-element.17) | data formatting | bytes 184320

commit v3 on v2

--- a/solution.py
+++ b/solution.py
@@ -19,6 +19,7 @@
 TAP_OF = [3 * slot % TAPS for slot in range(TAPS)]
 SLOTS = ((0, 2), (2, 2), (4, 1))
 STAGES = 3
+KEPT = ((0, 2, 3, 1), (0, 1, 2, 3))
 TILE = 256
 BLOCK_ROWS = (96, 32, 16)
 
@@ -53,8 +54,9 @@
     bases, up, table, weight, bias_in, gain_in, cot = take(7)
     ob, gi, gw, small = take(4)
     bases_e, up_e, cot_e, w_v, perm_v, permz_v, tab, xs, rin, hb, h5, hs, h_in, pre = take(14)
-    gbuf, gpar, g5, g5p, bsum, dh_a, dh_b, gws, bias, gain = take(10)
-    blocks, others, bias_blocks, bias_others = take(3), take(3), take(3), take(3)
+    gbuf, gpar, g5, g5p, bsum, dh, gws, bias, gain = take(9)
+    first_own, first_in, second_own, second_in = take(4)
+    blocks, others, bias_blocks, bias_others = [None, *take(2)], [None, *take(2)], take(3), take(3)
     wres = next(names)
     local_sem, send_sem, recv_sem = take(3)
 
@@ -110,9 +112,9 @@
         for b in range(C // 128):
             hit = column + b * 128 == channel + c * 48
             perm_v[n * HALF : (n + 1) * HALF, b * 128 : (b + 1) * 128] = hit.astype(F32).astype(BF)
-    kept = second * 96 + third * 24 + first * 6 + last
+    turned = second * 96 + third * 24 + first * 6 + last
     for b in range(HALF // 128):
-        permz_v[:, b * 128 : (b + 1) * 128] = (column + b * 128 == kept).astype(F32).astype(BF)
+        permz_v[:, b * 128 : (b + 1) * 128] = (column + b * 128 == turned).astype(F32).astype(BF)
 
     tab[...] = jnp.zeros(tab.shape, F32)
     tab[0:4, :] = table[...].astype(F32)
@@ -127,11 +129,11 @@
         r = lax.rsqrt(jnp.mean(x * x, axis=-1, keepdims=True) + 1e-06)
         return r, (x * r * gain[...])
 
-    def norm_block(b, carry):
-        e = embedded(b + 1)
-        for s in range(4):
-            row = pl.multiple_of(b * 128 + s * 32, 32)
-            x = up_e[pl.ds(row + HALO, 32), :].astype(F32) + e[s * 32 : s * 32 + 32]
+    def norm_block(pair, carry):
+        both = [embedded(2 * pair + 1), embedded(2 * pair + 2)]
+        for s in range(8):
+            row = pl.multiple_of(pair * 256 + s * 32, 32)
+            x = up_e[pl.ds(row + HALO, 32), :].astype(F32) + both[s // 4][s % 4 * 32 : s % 4 * 32 + 32]
             r, h = normed_of(x)
             xs[pl.ds(row, 32), :] = x
             rin[pl.ds(row, 32), :] = jnp.broadcast_to(r, (32, 128))
@@ -141,7 +143,7 @@
     def norm():
         for copy in (in_bases, in_up, *in_row):
             copy.wait()
-        lax.fori_loop(0, ROWS // 128, norm_block, 0)
+        lax.fori_loop(0, ROWS // 256, norm_block, 0)
         pl.semaphore_wait(barrier, len(partners))
         for copy in halos:
             copy.start()
@@ -192,16 +194,19 @@
         for n in range(GROUPS):
             pl.when(p == n)(in_w[n].wait)
         pl.when(p == 0)(in_cot.wait)
-        pre[...] = jnp.dot(h5[...], w_v[:, cols], preferred_element_type=F32)
-
-        def tile(i, carry):
-            row = times(i, 64)
-            act, slope = gelu_pair(pre[pl.ds(row + HALO, 64), :] + bias[:, cols])
-            ob[pl.ds(row, 64), cols] = (xs[pl.ds(row, 64), cols] + act).astype(BF)
-            gbuf[p, pl.ds(row + HALO, 64), :] = (cot_e[pl.ds(row + HALO, 64), cols].astype(F32) * slope).astype(BF)
-            return carry
-
-        lax.fori_loop(0, ROWS // 64, tile, 0)
+        half = EXT // 2
+
+        def tile(row, n):
+            act, slope = gelu_pair(pre[row + HALO : row + HALO + n, :] + bias[:, cols])
+            ob[row : row + n, cols] = (xs[row : row + n, cols] + act).astype(BF)
+            gbuf[p, row + HALO : row + HALO + n, :] = (cot_e[row + HALO : row + HALO + n, cols].astype(F32) * slope).astype(BF)
+
+        pre[0:half, :] = jnp.dot(h5[0:half, :], w_v[:, cols], preferred_element_type=F32)
+        for row in range(0, half - HALO, 64):
+            tile(row, 64)
+        pre[half:, :] = jnp.dot(h5[half:, :], w_v[:, cols], preferred_element_type=F32)
+        for row in range(half - HALO, ROWS, 64):
+            tile(row, 64)
         for side in range(2):
             rows = slice(side * (HALO + ROWS), side * (HALO + ROWS) + HALO)
             _, slope = gelu_pair(pre[rows, :] + bias[:, cols])
@@ -232,11 +237,28 @@
             copies.append(remote(first + delta - 1, source(along(axis) + delta), target(delta - 1), place(other, core)))
         return copies
 
+    def kept_set(c, odd):
+        return c >> 1 if odd else ((c + 1) >> 1) & 1
+
+    def mine_of(c, odd):
+        return c & 1 if odd else c >> 1
+
+    def pair_copy(p, slot, odd, step):
+        kind = lax.rem(p + lax.div(slot, 2), 3)
+        c = along(kind)
+        to = c ^ 1 if (step == 1) == odd else 3 - c
+        other = [jnp.where(kind == a, to, pos[a]) for a in range(3)]
+        n = 10 + (p * TAPS + slot) * 2 + step
+        if step == 0:
+            source = first_own.at[p, slot, pl.ds(2 * kept_set(to, odd), 2)]
+            return remote(n, source, first_in.at[p, slot], place(other, core))
+        return remote(n, second_own.at[p, slot], second_in.at[p, slot], place(other, core))
+
     def piece_hops(p, m, stage):
         slot, count = SLOTS[m]
         axis = axis_of(lax.rem(p + m, 3), stage)
         return hops(
-            10 + ((p * 3 + m) * STAGES + stage) * 3,
+            40 + ((p * 3 + m) * 2 + stage - 1) * 3,
             axis,
             lambda d: blocks[stage].at[p, lax.rem(d, 4), pl.ds(slot, count)],
             lambda d: others[stage].at[p, d, pl.ds(slot, count)],
@@ -244,7 +266,7 @@
 
     def bias_hops(stage):
         return hops(
-            10 + 27 * GROUPS + stage * 3,
+            10 + 28 * GROUPS + stage * 3,
             jnp.int32(stage),
             lambda d: bias_blocks[stage].at[lax.rem(d, 4)],
             lambda d: bias_others[stage].at[d],
@@ -266,41 +288,36 @@
             lhs = jnp.concatenate([hs[0], h_in[...]], axis=1)
             wres[:, 0 : count * WIDE] = jnp.dot(lhs, rhs, preferred_element_type=F32)
             kind = lax.rem(p + m, 3)
+            wide = count * WIDE
+
+            def store(block):
+                for d in range(4):
+                    rows = block(d).astype(BF)
+                    for n in range(count):
+                        first_own[p, first + n, KEPT[n][d]] = rows[:, n * WIDE : (n + 1) * WIDE]
+
+            @pl.when(kind == 0)
+            def _():
+                store(lambda d: wres[d * 96 : d * 96 + 96, 0:wide])
+
+            @pl.when(kind == 1)
+            def _():
+                store(lambda d: jnp.concatenate([wres[e * 96 + d * 24 : e * 96 + d * 24 + 24, 0:wide] for e in range(4)], axis=0))
+
+            @pl.when(kind == 2)
+            def _():
+                r = jnp.dot(permz_v[...], wres[:, 0:wide].astype(BF), preferred_element_type=F32)
+                store(lambda d: r[d * 96 : d * 96 + 96])
+
             for n in range(count):
-                cols = slice(n * WIDE, (n + 1) * WIDE)
-
-                def store(block):
-                    for d in range(4):
-                        blocks[0][p, d, first + n] = block(d).astype(BF)
-
-                @pl.when(kind == 0)
-                def _():
-                    store(lambda d: wres[d * 96 : d * 96 + 96, cols])
-
-                @pl.when(kind == 1)
-                def _():
-                    store(lambda d: jnp.concatenate([wres[e * 96 + d * 24 : e * 96 + d * 24 + 24, cols] for e in range(4)], axis=0))
-
-                @pl.when(kind == 2)
-                def _():
-                    r = jnp.dot(permz_v[...], wres[:, cols].astype(BF), preferred_element_type=F32)
-                    store(lambda d: r[d * 96 : d * 96 + 96])
+                pair_copy(p, first + n, n, 0).start()
 
         def pair(m, carry):
             piece(m, 2 * m, 2)
-            for n in range(2):
-
-                @pl.when(m == n)
-                def _():
-                    for copy in piece_hops(p, n, 0):
-                        copy.start()
-
             return carry
 
         lax.fori_loop(0, 2, pair, 0)
         piece(2, 4, 1)
-        for copy in piece_hops(p, 2, 0):
-            copy.start()
 
         @pl.when(p == GROUPS - 1)
         def _():
@@ -312,10 +329,12 @@
             for copy in bias_hops(0):
                 copy.start()
 
-    spread_row = lax.broadcasted_iota(jnp.int32, (64, 32), 0)
-    spread_col = lax.broadcasted_iota(jnp.int32, (64, 32), 1)
-    within = spread_row & 15
-    spread = ((within < 6) & (spread_col == 6 * (spread_row >> 4) + within)).astype(F32).astype(BF)
+    def spread_of(shape, sixteenth):
+        r, c = lax.broadcasted_iota(jnp.int32, shape, 0), lax.broadcasted_iota(jnp.int32, shape, 1)
+        return sixteenth(c, 6 * (r >> 4), r & 15).astype(F32).astype(BF)
+
+    spread = spread_of((64, 32), lambda c, base, w: (w < 6) & (c == base + w))
+    spread_two = spread_of((64, 48), lambda c, base, w: ((w & 7) < 6) & (c == base + (w & 7) + 24 * (w >> 3)))
 
     def handed_on(total, stage, store):
         if stage == 0:
@@ -327,7 +346,30 @@
             for d in range(4):
                 store(d, r[16 * d : 16 * d + 16])
 
-    def finish(p, stage):
+    def finish_first(p, step):
+        for m, (first, count) in enumerate(SLOTS):
+            c = along(lax.rem(p + m, 3))
+            for slot in range(first, first + count):
+                odd = slot % 2
+                pair_copy(p, slot, odd, step).wait_recv()
+                mine = mine_of(c, odd)
+                if step == 0:
+                    mine = 1 - mine
+                total = first_own[p, slot, 2 * kept_set(c, odd) + mine].astype(F32) + first_in[p, slot, mine].astype(F32)
+                if step == 0:
+                    second_own[p, slot, 0] = total.astype(BF)
+                    pair_copy(p, slot, odd, 1).start()
+                else:
+                    total = total + second_in[p, slot, 0].astype(F32)
+                    for d in range(4):
+                        rows = total[24 * d : 24 * d + 24]
+                        block = jnp.concatenate([rows[:, 0:128], rows[:, 128:]], axis=0)
+                        blocks[1][p, d, slot] = block.astype(BF)
+            if step == 1:
+                for copy in piece_hops(p, m, 1):
+                    copy.start()
+
+    def finish_next(p, stage):
         for m, (first, count) in enumerate(SLOTS):
             for copy in piece_hops(p, m, stage):
                 copy.wait_recv()
@@ -336,17 +378,22 @@
                 total = blocks[stage][p, own, slot].astype(F32)
                 for d in range(3):
                     total = total + others[stage][p, d, slot].astype(F32)
-                if stage == 2:
-                    gws[TAP_OF[slot], :, pl.ds(times(p, WIDE), WIDE)] = total[0:8]
+                if stage == 1:
+                    r = jnp.dot(spread_two, total.astype(BF), preferred_element_type=F32).astype(BF)
+                    for d in range(4):
+                        blocks[2][p, d, slot] = r[16 * d : 16 * d + 16]
                 else:
-
-                    def store(d, value):
-                        blocks[stage + 1][p, d, slot] = value
-
-                    handed_on(total, stage, store)
-            if stage < 2:
-                for copy in piece_hops(p, m, stage + 1):
+                    for half in range(2):
+                        gws[TAP_OF[slot], :, pl.ds(times(2 * p + half, 128), 128)] = total[8 * half : 8 * half + 8]
+            if stage == 1:
+                for copy in piece_hops(p, m, 2):
                     copy.start()
+
+    def finish(p, step):
+        if step < 2:
+            finish_first(p, step)
+        else:
+            finish_next(p, step - 1)
 
     def finish_bias(stage):
         for copy in bias_hops(stage):
@@ -372,7 +419,7 @@
             for k in range(TAPS)
         )
 
-    def input_gradient(t, dh):
+    def input_gradient(t):
         for i in range(TILE // 32):
             row = pl.multiple_of(t * TILE + i * 32, 32)
             r = jnp.concatenate([rin[pl.ds(row, 32), :]] * (C // 128), axis=1)
@@ -382,11 +429,9 @@
             g = cot_e[pl.ds(row + HALO, 32), :].astype(F32) + (dn - normed * mean) * r
             gi[pl.ds(row, 32), :] = g.astype(BF)
 
-    def backward(u):
-        dh_a[...] = hidden(2 * u)
-        input_gradient(jnp.maximum(2 * u - 1, 0), dh_b)
-        dh_b[...] = hidden(2 * u + 1)
-        input_gradient(2 * u, dh_a)
+    def backward(t):
+        input_gradient(jnp.maximum(t - 1, 0))
+        dh[...] = hidden(t)
 
     def during(s, start, stop, step):
         if stop > start:
@@ -395,21 +440,20 @@
     def turn_of(s, carry):
         during(s, 0, 3, lambda: forward(s))
         during(s, 1, 4, lambda: weights(s - 1))
-        during(s, 4, 6, lambda: backward(s - 4))
-        for stage in range(STAGES):
-            during(s, 2 + stage, 5 + stage, lambda: finish(s - 2 - stage, stage))
-            during(s, 4 + stage, 5 + stage, lambda: finish_bias(stage))
+        during(s, 4, 8, lambda: backward(s - 4))
+        for step in range(4):
+            during(s, 2 + step, 5 + step, lambda: finish(s - 2 - step, step))
+            if step < 3:
+                during(s, 5 + step, 6 + step, lambda: finish_bias(step))
         return carry
 
     norm()
     turn()
     norm_ends()
     shift_h()
-    dh_b[...] = jnp.zeros(dh_b.shape, F32)
-    lax.fori_loop(0, 6, turn_of, 0)
-    input_gradient(ROWS // TILE - 1, dh_b)
-    finish(2, 2)
-    finish_bias(2)
+    dh[...] = jnp.zeros(dh.shape, F32)
+    lax.fori_loop(0, 8, turn_of, 0)
+    input_gradient(ROWS // TILE - 1)
 
     gw[...] = gws[0:TAPS, 0:6, :]
     mine = (dp * 8 + seq) * 6
@@ -437,8 +481,11 @@
 
     def sent(p, carry):
         g_copy(p).wait_send()
+        for slot in range(TAPS):
+            for step in range(2):
+                pair_copy(p, slot, slot % 2, step).wait_send()
         for m in range(3):
-            for stage in range(STAGES):
+            for stage in (1, 2):
                 for copy in piece_hops(p, m, stage):
                     copy.wait_send()
         return carry
@@ -472,17 +519,17 @@
         pltpu.VMEM((ROWS, TAPS * WIDE), BF),
         pltpu.VMEM((8, C), F32),
         pltpu.VMEM((TILE, C), F32),
-        pltpu.VMEM((TILE, C), F32),
         pltpu.VMEM((TAPS + 1, 8, C), F32),
         pltpu.VMEM((1, C), F32),
         pltpu.VMEM((1, C), F32),
     ]
-    scratch += [pltpu.VMEM((GROUPS, 4, TAPS, rows, WIDE), BF) for rows in BLOCK_ROWS]
-    scratch += [pltpu.VMEM((GROUPS, 3, TAPS, rows, WIDE), BF) for rows in BLOCK_ROWS]
+    scratch += [pltpu.VMEM((GROUPS, TAPS, n, 96, WIDE), BF) for n in (4, 2, 1, 1)]
+    scratch += [pltpu.VMEM((GROUPS, 4, TAPS, rows, 128), BF) for rows in (48, 16)]
+    scratch += [pltpu.VMEM((GROUPS, 3, TAPS, rows, 128), BF) for rows in (48, 16)]
     scratch += [pltpu.VMEM((4, rows, 128), BF) for rows in BLOCK_ROWS]
     scratch += [pltpu.VMEM((3, rows, 128), BF) for rows in BLOCK_ROWS]
     scratch += [pltpu.VMEM((HALF, 2 * WIDE), F32)]
-    remotes = 10 + 27 * GROUPS + 9
+    remotes = 10 + 28 * GROUPS + 9
     scratch += [
         pltpu.SemaphoreType.DMA((16,)),
         pltpu.SemaphoreType.DMA((remotes,)),

time: 63.3 us -> 59.4 us (0.938)
  Pallas kernels: 59.1 us -> 55.1 us
    pallas_call x1, Pallas kernels: 59.1 us -> 55.1 us  [body(): pl.pallas_call(kernel, out_shape=[pltpu.VMEM((ROWS, C), BF), pltpu.VMEM((...]
where the time goes in v3:
time: 59.4 us; the launch traced here: 59.2 us
  Pallas kernels  55.1 us (93%)
  local copies, waits for them, and re-layouts  3.45 us (6%)
  between operations  0.64 us (1%)
    pallas_call x1, Pallas kernels, body(): pl.pallas_call(kernel, out_shape=[pltpu.VMEM((ROWS, C), BF), pltpu.VMEM((...  55.1 us
    unnamed x3, local copies, waits for them, and re-layouts  2.93 us

profile of v3, /device:TPU:0, one launch (start us, length us, event | category | flops | bytes accessed | tf_op | source)
XLA Modules:
  0.0 59.2 jit_solution(8514166835687831000)
XLA Ops:
  0.6 55.1 %block.1 = (bf16[1024,768]{1,0:T(8,128)(2,1)S(1)}, bf16[1024,768]{1,0:T(8,128)(2,1)S(1)}, f32[5,6,768]{2,1,0:T(8,128)S(1)}, f32[8,128]{1,0:T(8,128)S(1)}) custom-call(s32[1,1024]{1,0:T(1,128)} %refs_0_.1, bf16[1024,768]{1,0:T(8,128)(2,1)} %bitcast.12, bf16[4,768]{1,0:T(4,128)(2,1)} %refs_2_.1, bf16[3840,768]{1,0:T(8,128)(2,1)} %bitcast.11, f32[768]{0:T(1024)} %refs_4_.1, ...), custom_call_target="tpu_custom_call" | custom-call | tf_op jit(solution)/shard_map/block/pallas_call | solution.py:538
  55.7 0.5 slice_bitcast_fusion
  56.3 1.1 %copy.15 = bf16[1,1024,768]{2,1,0:T(8,128)(2,1)} copy(bf16[1,1024,768]{2,1,0:T(8,128)(2,1)S(1)} %bitcast.10) | data formatting | bytes 3145728
  57.4 1.1 %copy.16 = bf16[1,1024,768]{2,1,0:T(8,128)(2,1)} copy(bf16[1,1024,768]{2,1,0:T(8,128)(2,1)S(1)} %bitcast.9) | data formatting | bytes 3145728
  58.6 0.6 %copy.17 = f32[5,6,768]{2,1,0:T(8,128)} copy(f32[5,6,768]{2,1,0:T(8,128)S(1)} %get-tuple-element.17) | data formatting | bytes 184320

commit v4 on v3

--- a/solution.py
+++ b/solution.py
@@ -26,18 +26,17 @@
 
 def here():
     dp, seq = lax.axis_index("dp"), lax.axis_index("seq")
-    x = 2 * lax.div(dp, 8) + lax.rem(seq, 2)
-    return [x, lax.rem(lax.div(dp, 2), 4), lax.div(seq, 2)], lax.rem(dp, 2), dp, seq
+    return [2 * (dp >> 3) + (seq & 1), (dp >> 1) & 3, seq >> 1], dp & 1, dp, seq
 
 
 def place(pos, core):
     x, y, z = pos
-    return (lax.div(x, 2) * 8 + y * 2 + core, z * 2 + lax.rem(x, 2))
-
-
-def moved(pos, axis, delta):
+    return ((x >> 1) * 8 + y * 2 + core, z * 2 + (x & 1))
+
+
+def moved(pos, axis, to):
     other = list(pos)
-    other[axis] = lax.rem(pos[axis] + delta, 4)
+    other[axis] = to
     return other
 
 
@@ -62,7 +61,9 @@
 
     pos, core, dp, seq = here()
     partner = place(pos, 1 - core)
-    left, right = (dp, lax.rem(seq + 7, 8)), (dp, lax.rem(seq + 1, 8))
+    left, right = (dp, (seq + 7) & 7), (dp, (seq + 1) & 7)
+    onward = {n: [place(moved(pos, a, (pos[a] + n) & 3), core) for a in range(3)] for n in (1, 2, 3)}
+    beside = [[place(moved(pos, a, to(pos[a])), core) for a in range(3)] for to in (lambda c: c ^ 1, lambda c: 3 - c)]
     inside = (seq > 0, seq < 7)
 
     def remote(n, src, dst, device):
@@ -84,7 +85,7 @@
 
     barrier = pltpu.get_barrier_semaphore()
     partners = [partner, left, right]
-    partners += [place(moved(pos, axis, delta), core) for axis in range(3) for delta in (1, 2, 3)]
+    partners += [device for devices in onward.values() for device in devices]
     for device in partners:
         pl.semaphore_signal(barrier, inc=1, device_id=device, device_id_type=MESH)
 
@@ -160,14 +161,13 @@
             hb[start + HALO : start + 2 * HALO, :] = h.astype(BF)
 
     def turn():
-        def one(n, carry):
-            rows = perm_v[pl.ds(times(1 - n, HALF), HALF), :]
+        for n in range(2):
+            rows = perm_v[(1 - n) * HALF : (2 - n) * HALF, :]
             h_own = hb[2 * HALO : 2 * HALO + ROWS, :]
             hs[1 - n] = lax.dot_general(rows, h_own, NT, preferred_element_type=F32).astype(BF)
-            pl.when(n == 0)(h_copy.start)
-            return carry
-
-        lax.fori_loop(0, 2, one, 0)
+            if n == 0:
+                h_copy.start()
+
 
     def shift_h():
         def tile(j, carry):
@@ -227,15 +227,30 @@
     def axis_of(kind, stage):
         return (kind, jnp.where(kind == 0, 1, 0), jnp.where(kind == 2, 1, 2))[stage]
 
+    def pick_of(axis, three):
+        return jnp.where(axis == 0, three[0], jnp.where(axis == 1, three[1], three[2]))
+
     def along(axis):
-        return jnp.where(axis == 0, pos[0], jnp.where(axis == 1, pos[1], pos[2]))
-
-    def hops(first, axis, source, target):
-        copies = []
-        for delta in (1, 2, 3):
-            other = [lax.rem(pos[a] + jnp.where(axis == a, delta, 0), 4) for a in range(3)]
-            copies.append(remote(first + delta - 1, source(along(axis) + delta), target(delta - 1), place(other, core)))
-        return copies
+        return pick_of(axis, pos)
+
+    def device_of(axis, three):
+        return tuple(pick_of(axis, [device[n] for device in three]) for n in range(2))
+
+    def kind_of(p, m):
+        return jnp.where(p + m >= 3, p + m - 3, p + m)
+
+    def step_sem(p, step):
+        return 10 + 4 * p + step
+
+    def step_wait(p, step):
+        whole = (first_in, second_in, others[1], others[2])[step].at[p]
+        return remote(step_sem(p, step), whole, whole, partner)
+
+    def hops(n, axis, source, target):
+        c = along(axis)
+        return [
+            remote(n, source((c + delta) & 3), target(delta - 1), device_of(axis, onward[delta])) for delta in (1, 2, 3)
+        ]
 
     def kept_set(c, odd):
         return c >> 1 if odd else ((c + 1) >> 1) & 1
@@ -243,34 +258,36 @@
     def mine_of(c, odd):
         return c & 1 if odd else c >> 1
 
-    def pair_copy(p, slot, odd, step):
-        kind = lax.rem(p + lax.div(slot, 2), 3)
+    def pair_copy(p, m, n, step):
+        kind, slot, odd = kind_of(p, m), 2 * m + n, n
         c = along(kind)
-        to = c ^ 1 if (step == 1) == odd else 3 - c
-        other = [jnp.where(kind == a, to, pos[a]) for a in range(3)]
-        n = 10 + (p * TAPS + slot) * 2 + step
+        flip = (step == 0) == (odd == 0)
+        other = device_of(kind, beside[0 if flip else 1])
         if step == 0:
+            to = c ^ 1 if flip else 3 - c
             source = first_own.at[p, slot, pl.ds(2 * kept_set(to, odd), 2)]
-            return remote(n, source, first_in.at[p, slot], place(other, core))
-        return remote(n, second_own.at[p, slot], second_in.at[p, slot], place(other, core))
+            return remote(step_sem(p, step), source, first_in.at[p, slot], other)
+        return remote(step_sem(p, step), second_own.at[p, slot], second_in.at[p, slot], other)
 
     def piece_hops(p, m, stage):
         slot, count = SLOTS[m]
-        axis = axis_of(lax.rem(p + m, 3), stage)
         return hops(
-            40 + ((p * 3 + m) * 2 + stage - 1) * 3,
-            axis,
-            lambda d: blocks[stage].at[p, lax.rem(d, 4), pl.ds(slot, count)],
+            step_sem(p, stage + 1),
+            axis_of(kind_of(p, m), stage),
+            lambda d: blocks[stage].at[p, d, pl.ds(slot, count)],
             lambda d: others[stage].at[p, d, pl.ds(slot, count)],
         )
 
     def bias_hops(stage):
         return hops(
-            10 + 28 * GROUPS + stage * 3,
+            22 + stage,
             jnp.int32(stage),
-            lambda d: bias_blocks[stage].at[lax.rem(d, 4)],
+            lambda d: bias_blocks[stage].at[d],
             lambda d: bias_others[stage].at[d],
         )
+
+    def bias_wait(stage):
+        return remote(22 + stage, bias_others[stage], bias_others[stage], partner)
 
     def weights(p):
         shift_g(gbuf, p, g5, lambda k: pl.multiple_of(k * C + p * WIDE, WIDE))
@@ -287,7 +304,7 @@
             rhs = jnp.concatenate([jnp.concatenate(own, axis=1) if count > 1 else own[0], other], axis=0)
             lhs = jnp.concatenate([hs[0], h_in[...]], axis=1)
             wres[:, 0 : count * WIDE] = jnp.dot(lhs, rhs, preferred_element_type=F32)
-            kind = lax.rem(p + m, 3)
+            kind = kind_of(p, m)
             wide = count * WIDE
 
             def store(block):
@@ -310,7 +327,7 @@
                 store(lambda d: r[d * 96 : d * 96 + 96])
 
             for n in range(count):
-                pair_copy(p, first + n, n, 0).start()
+                pair_copy(p, m, n, 0).start()
 
         def pair(m, carry):
             piece(m, 2 * m, 2)
@@ -347,18 +364,18 @@
                 store(d, r[16 * d : 16 * d + 16])
 
     def finish_first(p, step):
+        step_wait(p, step).wait_recv()
         for m, (first, count) in enumerate(SLOTS):
-            c = along(lax.rem(p + m, 3))
+            c = along(kind_of(p, m))
             for slot in range(first, first + count):
                 odd = slot % 2
-                pair_copy(p, slot, odd, step).wait_recv()
                 mine = mine_of(c, odd)
                 if step == 0:
                     mine = 1 - mine
                 total = first_own[p, slot, 2 * kept_set(c, odd) + mine].astype(F32) + first_in[p, slot, mine].astype(F32)
                 if step == 0:
                     second_own[p, slot, 0] = total.astype(BF)
-                    pair_copy(p, slot, odd, 1).start()
+                    pair_copy(p, m, odd, 1).start()
                 else:
                     total = total + second_in[p, slot, 0].astype(F32)
                     for d in range(4):
@@ -370,10 +387,9 @@
                     copy.start()
 
     def finish_next(p, stage):
+        step_wait(p, stage + 1).wait_recv()
         for m, (first, count) in enumerate(SLOTS):
-            for copy in piece_hops(p, m, stage):
-                copy.wait_recv()
-            own = along(axis_of(lax.rem(p + m, 3), stage))
+            own = along(axis_of(kind_of(p, m), stage))
             for slot in range(first, first + count):
                 total = blocks[stage][p, own, slot].astype(F32)
                 for d in range(3):
@@ -396,8 +412,7 @@
             finish_next(p, step - 1)
 
     def finish_bias(stage):
-        for copy in bias_hops(stage):
-            copy.wait_recv()
+        bias_wait(stage).wait_recv()
         total = bias_blocks[stage][pos[stage]].astype(F32)
         for d in range(3):
             total = total + bias_others[stage][d].astype(F32)
@@ -457,7 +472,7 @@
 
     gw[...] = gws[0:TAPS, 0:6, :]
     mine = (dp * 8 + seq) * 6
-    base = jnp.minimum(lax.div(mine, 16) * 16, C - 32)
+    base = jnp.minimum((mine >> 4) * 16, C - 32)
     pick_row = lax.broadcasted_iota(jnp.int32, (8, 32), 0)
     pick_col = lax.broadcasted_iota(jnp.int32, (8, 32), 1)
     pick = (pick_col == pick_row + (mine - base)).astype(F32).astype(BF)
@@ -476,18 +491,12 @@
     for copy in (*halos, h_copy):
         copy.wait_send()
     for stage in range(STAGES):
-        for copy in bias_hops(stage):
-            copy.wait_send()
+        bias_wait(stage).wait_send()
 
     def sent(p, carry):
         g_copy(p).wait_send()
-        for slot in range(TAPS):
-            for step in range(2):
-                pair_copy(p, slot, slot % 2, step).wait_send()
-        for m in range(3):
-            for stage in (1, 2):
-                for copy in piece_hops(p, m, stage):
-                    copy.wait_send()
+        for step in range(4):
+            step_wait(p, step).wait_send()
         return carry
 
     lax.fori_loop(0, GROUPS, sent, 0)
@@ -529,7 +538,7 @@
     scratch += [pltpu.VMEM((4, rows, 128), BF) for rows in BLOCK_ROWS]
     scratch += [pltpu.VMEM((3, rows, 128), BF) for rows in BLOCK_ROWS]
     scratch += [pltpu.VMEM((HALF, 2 * WIDE), F32)]
-    remotes = 10 + 28 * GROUPS + 9
+    remotes = 10 + 4 * GROUPS + STAGES
     scratch += [
         pltpu.SemaphoreType.DMA((16,)),
         pltpu.SemaphoreType.DMA((remotes,)),

time: 59.4 us -> 58.1 us (0.978)
  Pallas kernels: 55.1 us -> 53.8 us
    pallas_call x1, Pallas kernels: 55.1 us -> 53.8 us  [body(): pl.pallas_call(kernel, out_shape=[pltpu.VMEM((ROWS, C), BF), pltpu.VMEM((...]
where the time goes in v4:
time: 58.1 us; the launch traced here: 57.9 us
  Pallas kernels  53.8 us (93%)
  local copies, waits for them, and re-layouts  3.45 us (6%)
  between operations  0.64 us (1%)
    pallas_call x1, Pallas kernels, body(): pl.pallas_call(kernel, out_shape=[pltpu.VMEM((ROWS, C), BF), pltpu.VMEM((...  53.8 us
    unnamed x3, local copies, waits for them, and re-layouts  2.93 us

profile of v4, /device:TPU:0, one launch (start us, length us, event | category | flops | bytes accessed | tf_op | source)
XLA Modules:
  0.0 57.9 jit_solution(369814485696588214)
XLA Ops:
  0.6 53.8 %block.1 = (bf16[1024,768]{1,0:T(8,128)(2,1)S(1)}, bf16[1024,768]{1,0:T(8,128)(2,1)S(1)}, f32[5,6,768]{2,1,0:T(8,128)S(1)}, f32[8,128]{1,0:T(8,128)S(1)}) custom-call(s32[1,1024]{1,0:T(1,128)} %refs_0_.1, bf16[1024,768]{1,0:T(8,128)(2,1)} %bitcast.12, bf16[4,768]{1,0:T(4,128)(2,1)} %refs_2_.1, bf16[3840,768]{1,0:T(8,128)(2,1)} %bitcast.11, f32[768]{0:T(1024)} %refs_4_.1, ...), custom_call_target="tpu_custom_call" | custom-call | tf_op jit(solution)/shard_map/block/pallas_call | solution.py:547
  54.5 0.5 slice_bitcast_fusion
  55.0 1.1 %copy.15 = bf16[1,1024,768]{2,1,0:T(8,128)(2,1)} copy(bf16[1,1024,768]{2,1,0:T(8,128)(2,1)S(1)} %bitcast.10) | data formatting | bytes 3145728
  56.1 1.1 %copy.16 = bf16[1,1024,768]{2,1,0:T(8,128)(2,1)} copy(bf16[1,1024,768]{2,1,0:T(8,128)(2,1)S(1)} %bitcast.9) | data formatting | bytes 3145728
  57.3 0.6 %copy.17 = f32[5,6,768]{2,1,0:T(8,128)} copy(f32[5,6,768]{2,1,0:T(8,128)S(1)} %get-tuple-element.17) | data formatting | bytes 184320

commit v5 on v4

--- a/solution.py
+++ b/solution.py
@@ -56,7 +56,7 @@
     gbuf, gpar, g5, g5p, bsum, dh, gws, bias, gain = take(9)
     first_own, first_in, second_own, second_in = take(4)
     blocks, others, bias_blocks, bias_others = [None, *take(2)], [None, *take(2)], take(3), take(3)
-    wres = next(names)
+    wres, mid, swap_v = take(3)
     local_sem, send_sem, recv_sem = take(3)
 
     pos, core, dp, seq = here()
@@ -117,7 +117,11 @@
     for b in range(HALF // 128):
         permz_v[:, b * 128 : (b + 1) * 128] = (column + b * 128 == turned).astype(F32).astype(BF)
 
+    swapped = ((sixth & 3) * 24 + ((sixth >> 2) & 3) * 6 + last)[0:96]
+    swap_v[...] = (column[0:96] == swapped).astype(F32).astype(BF)
+
     tab[...] = jnp.zeros(tab.shape, F32)
+    mid[...] = jnp.zeros(mid.shape, F32)
     tab[0:4, :] = table[...].astype(F32)
     bsum[...] = jnp.zeros(bsum.shape, F32)
     code = lax.broadcasted_iota(jnp.int32, (8, 128), 0)
@@ -225,7 +229,7 @@
         bsum[:, pl.ds(times(p, WIDE), WIDE)] += lax.fori_loop(0, ROWS // 128, tile, jnp.zeros((8, WIDE), F32))
 
     def axis_of(kind, stage):
-        return (kind, jnp.where(kind == 0, 1, 0), jnp.where(kind == 2, 1, 2))[stage]
+        return jnp.where(kind + stage >= 3, kind + stage - 3, kind + stage)
 
     def pick_of(axis, three):
         return jnp.where(axis == 0, three[0], jnp.where(axis == 1, three[1], three[2]))
@@ -377,9 +381,14 @@
                     second_own[p, slot, 0] = total.astype(BF)
                     pair_copy(p, m, odd, 1).start()
                 else:
-                    total = total + second_in[p, slot, 0].astype(F32)
+                    mid[0:96, :] = total + second_in[p, slot, 0].astype(F32)
+
+                    @pl.when(kind_of(p, m) == 1)
+                    def _():
+                        mid[0:96, :] = jnp.dot(swap_v[...], mid[...].astype(BF), preferred_element_type=F32)
+
                     for d in range(4):
-                        rows = total[24 * d : 24 * d + 24]
+                        rows = mid[24 * d : 24 * d + 24, :]
                         block = jnp.concatenate([rows[:, 0:128], rows[:, 128:]], axis=0)
                         blocks[1][p, d, slot] = block.astype(BF)
             if step == 1:
@@ -537,7 +546,7 @@
     scratch += [pltpu.VMEM((GROUPS, 3, TAPS, rows, 128), BF) for rows in (48, 16)]
     scratch += [pltpu.VMEM((4, rows, 128), BF) for rows in BLOCK_ROWS]
     scratch += [pltpu.VMEM((3, rows, 128), BF) for rows in BLOCK_ROWS]
-    scratch += [pltpu.VMEM((HALF, 2 * WIDE), F32)]
+    scratch += [pltpu.VMEM((HALF, 2 * WIDE), F32), pltpu.VMEM((128, WIDE), F32), pltpu.VMEM((96, 128), BF)]
     remotes = 10 + 4 * GROUPS + STAGES
     scratch += [
         pltpu.SemaphoreType.DMA((16,)),

time: 58.1 us -> 56.8 us (0.978)
  Pallas kernels: 53.8 us -> 52.5 us
    pallas_call x1, Pallas kernels: 53.8 us -> 52.5 us  [body(): pl.pallas_call(kernel, out_shape=[pltpu.VMEM((ROWS, C), BF), pltpu.VMEM((...]
where the time goes in v5:
time: 56.8 us; the launch traced here: 56.6 us
  Pallas kernels  52.5 us (92%)
  local copies, waits for them, and re-layouts  3.45 us (6%)
  between operations  0.64 us (1%)
    pallas_call x1, Pallas kernels, body(): pl.pallas_call(kernel, out_shape=[pltpu.VMEM((ROWS, C), BF), pltpu.VMEM((...  52.5 us
    unnamed x3, local copies, waits for them, and re-layouts  2.93 us

profile of v5, /device:TPU:0, one launch (start us, length us, event | category | flops | bytes accessed | tf_op | source)
XLA Modules:
  0.0 56.6 jit_solution(14076719758791210267)
XLA Ops:
  0.6 52.5 %block.1 = (bf16[1024,768]{1,0:T(8,128)(2,1)S(1)}, bf16[1024,768]{1,0:T(8,128)(2,1)S(1)}, f32[5,6,768]{2,1,0:T(8,128)S(1)}, f32[8,128]{1,0:T(8,128)S(1)}) custom-call(s32[1,1024]{1,0:T(1,128)} %refs_0_.1, bf16[1024,768]{1,0:T(8,128)(2,1)} %bitcast.12, bf16[4,768]{1,0:T(4,128)(2,1)} %refs_2_.1, bf16[3840,768]{1,0:T(8,128)(2,1)} %bitcast.11, f32[768]{0:T(1024)} %refs_4_.1, ...), custom_call_target="tpu_custom_call" | custom-call | tf_op jit(solution)/shard_map/block/pallas_call | solution.py:556
  53.2 0.5 slice_bitcast_fusion
  53.7 1.1 %copy.15 = bf16[1,1024,768]{2,1,0:T(8,128)(2,1)} copy(bf16[1,1024,768]{2,1,0:T(8,128)(2,1)S(1)} %bitcast.10) | data formatting | bytes 3145728
  54.8 1.1 %copy.16 = bf16[1,1024,768]{2,1,0:T(8,128)(2,1)} copy(bf16[1,1024,768]{2,1,0:T(8,128)(2,1)S(1)} %bitcast.9) | data formatting | bytes 3145728
  56.0 0.6 %copy.17 = f32[5,6,768]{2,1,0:T(8,128)} copy(f32[5,6,768]{2,1,0:T(8,128)S(1)} %get-tuple-element.17) | data formatting | bytes 184320

commit v6 on v5

--- a/solution.py
+++ b/solution.py
@@ -56,7 +56,7 @@
     gbuf, gpar, g5, g5p, bsum, dh, gws, bias, gain = take(9)
     first_own, first_in, second_own, second_in = take(4)
     blocks, others, bias_blocks, bias_others = [None, *take(2)], [None, *take(2)], take(3), take(3)
-    wres, mid, swap_v = take(3)
+    wres, mid, swap_v, w_own = take(4)
     local_sem, send_sem, recv_sem = take(3)
 
     pos, core, dp, seq = here()
@@ -80,7 +80,7 @@
     in_row = [local(2, bias_in, bias.at[0]), local(3, gain_in, gain.at[0])]
     in_w = [local(6 + p, weight.at[:, pl.ds(p * WIDE, WIDE)], w_v.at[:, pl.ds(p * WIDE, WIDE)]) for p in range(GROUPS)]
     in_cot = local(9, cot, cot_e.at[pl.ds(HALO, ROWS)])
-    for copy in (in_bases, in_up, *in_row, *in_w, in_cot):
+    for copy in (in_bases, in_up, *in_row):
         copy.start()
 
     barrier = pltpu.get_barrier_semaphore()
@@ -148,6 +148,8 @@
     def norm():
         for copy in (in_bases, in_up, *in_row):
             copy.wait()
+        for copy in (*in_w, in_cot):
+            copy.start()
         lax.fori_loop(0, ROWS // 256, norm_block, 0)
         pl.semaphore_wait(barrier, len(partners))
         for copy in halos:
@@ -457,6 +459,27 @@
         input_gradient(jnp.maximum(t - 1, 0))
         dh[...] = hidden(t)
 
+    mine = (dp * 8 + seq) * 6
+
+    def own_weights():
+        base = jnp.minimum((mine >> 4) * 16, C - 32)
+        pick_row = lax.broadcasted_iota(jnp.int32, (8, 32), 0)
+        pick_col = lax.broadcasted_iota(jnp.int32, (8, 32), 1)
+        pick = (pick_col == pick_row + (mine - base)).astype(F32).astype(BF)
+        for k in range(TAPS):
+            rows = w_v[pl.ds(pl.multiple_of(k * C + base, 16), 32), :]
+            w_own[k] = jnp.dot(pick, rows, preferred_element_type=F32)
+
+    def before_last():
+        input_gradient(ROWS // TILE - 1)
+        for copy in (*halos, h_copy):
+            copy.wait_send()
+        for p in range(GROUPS):
+            g_copy(p).wait_send()
+        for p in range(GROUPS - 1):
+            for step in range(4):
+                step_wait(p, step).wait_send()
+
     def during(s, start, stop, step):
         if stop > start:
             pl.when((s >= start) & (s < stop))(step)
@@ -465,6 +488,8 @@
         during(s, 0, 3, lambda: forward(s))
         during(s, 1, 4, lambda: weights(s - 1))
         during(s, 4, 8, lambda: backward(s - 4))
+        during(s, 6, 7, own_weights)
+        during(s, 7, 8, before_last)
         for step in range(4):
             during(s, 2 + step, 5 + step, lambda: finish(s - 2 - step, step))
             if step < 3:
@@ -477,18 +502,11 @@
     shift_h()
     dh[...] = jnp.zeros(dh.shape, F32)
     lax.fori_loop(0, 8, turn_of, 0)
-    input_gradient(ROWS // TILE - 1)
 
     gw[...] = gws[0:TAPS, 0:6, :]
-    mine = (dp * 8 + seq) * 6
-    base = jnp.minimum((mine >> 4) * 16, C - 32)
-    pick_row = lax.broadcasted_iota(jnp.int32, (8, 32), 0)
-    pick_col = lax.broadcasted_iota(jnp.int32, (8, 32), 1)
-    pick = (pick_col == pick_row + (mine - base)).astype(F32).astype(BF)
     total = jnp.zeros((8, C), F32)
     for k in range(TAPS):
-        rows = w_v[pl.ds(pl.multiple_of(k * C + base, 16), 32), :]
-        total = total + jnp.dot(pick, rows, preferred_element_type=F32) * gws[k]
+        total = total + w_own[k] * gws[k]
     lane = lax.broadcasted_iota(jnp.int32, (8, C), 1)
     row = lax.broadcasted_iota(jnp.int32, (8, C), 0)
     own_gain = jnp.sum(jnp.where(lane == row + mine, gain[...], 0.0), axis=-1, keepdims=True)
@@ -497,18 +515,10 @@
     small[0:1, :] = jnp.sum(jnp.where(diagonal, gws[TAPS, :, 0:128], 0.0), axis=0, keepdims=True)
     small[1:2, :] = jnp.sum(jnp.where(diagonal, column, 0.0), axis=0, keepdims=True)
 
-    for copy in (*halos, h_copy):
-        copy.wait_send()
     for stage in range(STAGES):
         bias_wait(stage).wait_send()
-
-    def sent(p, carry):
-        g_copy(p).wait_send()
-        for step in range(4):
-            step_wait(p, step).wait_send()
-        return carry
-
-    lax.fori_loop(0, GROUPS, sent, 0)
+    for step in range(4):
+        step_wait(GROUPS - 1, step).wait_send()
 
 
 MESH = pl.DeviceIdType.MESH
@@ -547,6 +557,7 @@
     scratch += [pltpu.VMEM((4, rows, 128), BF) for rows in BLOCK_ROWS]
     scratch += [pltpu.VMEM((3, rows, 128), BF) for rows in BLOCK_ROWS]
     scratch += [pltpu.VMEM((HALF, 2 * WIDE), F32), pltpu.VMEM((128, WIDE), F32), pltpu.VMEM((96, 128), BF)]
+    scratch += [pltpu.VMEM((TAPS, 8, C), F32)]
     remotes = 10 + 4 * GROUPS + STAGES
     scratch += [
         pltpu.SemaphoreType.DMA((16,)),

time: 56.8 us -> 56.6 us (level)
  no operation moved by 1% of the time
where the time goes in v6:
time: 56.6 us; the launch traced here: 56.4 us
  Pallas kernels  52.3 us (92%)
  local copies, waits for them, and re-layouts  3.45 us (6%)
  between operations  0.64 us (1%)
    pallas_call x1, Pallas kernels, body(): pl.pallas_call(kernel, out_shape=[pltpu.VMEM((ROWS, C), BF), pltpu.VMEM((...  52.3 us
    unnamed x3, local copies, waits for them, and re-layouts  2.93 us

profile of v6, /device:TPU:0, one launch (start us, length us, event | category | flops | bytes accessed | tf_op | source)
XLA Modules:
  0.0 56.4 jit_solution(11550287586322500579)
XLA Ops:
  0.6 52.3 %block.1 = (bf16[1024,768]{1,0:T(8,128)(2,1)S(1)}, bf16[1024,768]{1,0:T(8,128)(2,1)S(1)}, f32[5,6,768]{2,1,0:T(8,128)S(1)}, f32[8,128]{1,0:T(8,128)S(1)}) custom-call(s32[1,1024]{1,0:T(1,128)} %refs_0_.1, bf16[1024,768]{1,0:T(8,128)(2,1)} %bitcast.12, bf16[4,768]{1,0:T(4,128)(2,1)} %refs_2_.1, bf16[3840,768]{1,0:T(8,128)(2,1)} %bitcast.11, f32[768]{0:T(1024)} %refs_4_.1, ...), custom_call_target="tpu_custom_call" | custom-call | tf_op jit(solution)/shard_map/block/pallas_call | solution.py:567
  52.9 0.5 slice_bitcast_fusion
  53.5 1.1 %copy.15 = bf16[1,1024,768]{2,1,0:T(8,128)(2,1)} copy(bf16[1,1024,768]{2,1,0:T(8,128)(2,1)S(1)} %bitcast.10) | data formatting | bytes 3145728
  54.6 1.1 %copy.16 = bf16[1,1024,768]{2,1,0:T(8,128)(2,1)} copy(bf16[1,1024,768]{2,1,0:T(8,128)(2,1)S(1)} %bitcast.9) | data formatting | bytes 3145728
  55.7 0.6 %copy.17 = f32[5,6,768]{2,1,0:T(8,128)} copy(f32[5,6,768]{2,1,0:T(8,128)S(1)} %get-tuple-element.17) | data formatting | bytes 184320

commit v7 on v6

--- a/solution.py
+++ b/solution.py
@@ -486,12 +486,18 @@
 
     def turn_of(s, carry):
         during(s, 0, 3, lambda: forward(s))
+        during(s, 2, 3, lambda: finish(0, 0))
+        during(s, 3, 4, lambda: finish(0, 1))
         during(s, 1, 4, lambda: weights(s - 1))
         during(s, 4, 8, lambda: backward(s - 4))
         during(s, 6, 7, own_weights)
         during(s, 7, 8, before_last)
         for step in range(4):
-            during(s, 2 + step, 5 + step, lambda: finish(s - 2 - step, step))
+            now = (s >= 3 + step) & (s < 5 + step)
+            if step < 2:
+                pl.when(now)(lambda: finish(s - 2 - step, step))
+            else:
+                pl.when(now | (s == 1 + step))(lambda: finish(jnp.maximum(s - 2 - step, 0), step))
             if step < 3:
                 during(s, 5 + step, 6 + step, lambda: finish_bias(step))
         return carry

time: 56.6 us -> 56.4 us (level)
  no operation moved by 1% of the time
where the time goes in v7:
time: 56.4 us; the launch traced here: 56.3 us
  Pallas kernels  52.2 us (93%)
  local copies, waits for them, and re-layouts  3.45 us (6%)
  between operations  0.64 us (1%)
    pallas_call x1, Pallas kernels, body(): pl.pallas_call(kernel, out_shape=[pltpu.VMEM((ROWS, C), BF), pltpu.VMEM((...  52.2 us
    unnamed x3, local copies, waits for them, and re-layouts  2.93 us

profile of v7, /device:TPU:0, one launch (start us, length us, event | category | flops | bytes accessed | tf_op | source)
XLA Modules:
  0.0 56.3 jit_solution(12026395816865390032)
XLA Ops:
  0.6 52.2 %block.1 = (bf16[1024,768]{1,0:T(8,128)(2,1)S(1)}, bf16[1024,768]{1,0:T(8,128)(2,1)S(1)}, f32[5,6,768]{2,1,0:T(8,128)S(1)}, f32[8,128]{1,0:T(8,128)S(1)}) custom-call(s32[1,1024]{1,0:T(1,128)} %refs_0_.1, bf16[1024,768]{1,0:T(8,128)(2,1)} %bitcast.12, bf16[4,768]{1,0:T(4,128)(2,1)} %refs_2_.1, bf16[3840,768]{1,0:T(8,128)(2,1)} %bitcast.11, f32[768]{0:T(1024)} %refs_4_.1, ...), custom_call_target="tpu_custom_call" | custom-call | tf_op jit(solution)/shard_map/block/pallas_call | solution.py:573
  52.8 0.5 slice_bitcast_fusion
  53.3 1.1 %copy.15 = bf16[1,1024,768]{2,1,0:T(8,128)(2,1)} copy(bf16[1,1024,768]{2,1,0:T(8,128)(2,1)S(1)} %bitcast.10) | data formatting | bytes 3145728
  54.5 1.1 %copy.16 = bf16[1,1024,768]{2,1,0:T(8,128)(2,1)} copy(bf16[1,1024,768]{2,1,0:T(8,128)(2,1)S(1)} %bitcast.9) | data formatting | bytes 3145728
  55.6 0.6 %copy.17 = f32[5,6,768]{2,1,0:T(8,128)} copy(f32[5,6,768]{2,1,0:T(8,128)S(1)} %get-tuple-element.17) | data formatting | bytes 184320
